TPU v7x, 128 devices: a whole 4x4x4 slice. The times are simulated.
128 devices in a mesh: dp: 16 (over x, z), cent: 8 (over y, core).
Axes of the slice: x: 4, y: 4, z: 4, core: 2. Of those that a mesh axis runs over, the one named last changes fastest.
Arguments:
- embeddings: bfloat16 [16384, 4096], P('dp'), may hold values from -15 to 15
- centroids: bfloat16 [8192, 4096], P('cent', 'dp'), may hold values from -12 to 12
Outputs:
- shares: bfloat16 [16384, 8192], P('dp', 'cent')
- new_centroids: bfloat16 [8192, 4096], P('cent', 'dp')
All inputs are finite; a program needn't handle non-finite values.
Results may differ from a plain program's by a relative error of at most 0.0034.
Values may be sent and summed in bfloat16 or wider, within the bound.
No kernel may reach another device: no remote copies, remote signals or barrier semaphores. Data moves between devices by JAX's collectives and lax.ppermute only.
A program may use at most 128 MiB of HBM per device.

v0:
```python
import functools

import jax
import jax.numpy as jnp
from jax import lax
from jax.experimental import pallas as pl
from jax.experimental.pallas import tpu as pltpu
from jax.sharding import PartitionSpec as P

ROUNDS = 3
SIDE = 4
PACK = 0.25
MASS_ROWS = 16


def _x(step):
    return [
        (x * SIDE + z, ((x + step) % SIDE) * SIDE + z) for x in range(SIDE) for z in range(SIDE)
    ]


def _z(step):
    return [
        (x * SIDE + z, x * SIDE + (z + step) % SIDE) for x in range(SIDE) for z in range(SIDE)
    ]


def _send(value, axis, step):
    return lax.ppermute(value, "dp", axis(step))


def _dot_rows(rows, block):
    return lax.dot_general(
        block, rows, (((1,), (1,)), ((), ())), preferred_element_type=jnp.float32
    )


def _squares(block):
    wide = block.astype(jnp.float32)
    return jnp.sum(wide * wide, 1)


def _ring(block, axis):
    before, after = _send(block, axis, 1), _send(block, axis, -1)
    half = block.shape[0] // 2
    low, high = _send(before[:half], axis, 1), _send(after[half:], axis, -1)
    return after, jnp.concatenate([low, high], 0), before


def _line_panel(axis, block):
    return jnp.concatenate([block, *_ring(block, axis)], 1)


def _near_scores_kernel(total_ref, after_ref, before_ref, rows_1_ref, rows_3_ref, out_ref):
    out_ref[...] = (
        total_ref[...]
        + _dot_rows(rows_1_ref[...], after_ref[...])
        + _dot_rows(rows_3_ref[...], before_ref[...])
    )


def _near_scores(total, after, before, rows):
    count, wide = after.shape
    tile = rows.shape[0] // SIDE
    panel = pl.BlockSpec((count, wide), lambda i: (0, 0))
    tiles = pl.BlockSpec((count, tile), lambda i: (0, i))
    return pl.pallas_call(
        _near_scores_kernel,
        grid=(SIDE,),
        in_specs=[
            tiles,
            panel,
            panel,
            pl.BlockSpec((tile, wide), lambda i: (i, 1)),
            pl.BlockSpec((tile, wide), lambda i: (i, 3)),
        ],
        out_specs=tiles,
        out_shape=jax.ShapeDtypeStruct(total.shape, jnp.float32),
        cost_estimate=pl.CostEstimate(
            flops=4 * count * wide * rows.shape[0],
            bytes_accessed=4 * wide * (count + rows.shape[0]) + 8 * total.size,
            transcendentals=0,
        ),
        compiler_params=pltpu.CompilerParams(vmem_limit_bytes=14 * 1024 * 1024),
    )(total, after, before, rows, rows)


def _gather_scores(axis, panel, rows):
    after, far, before = _ring(panel, axis)
    wide = panel.shape[1]
    total = _dot_rows(rows[:, :wide], panel)
    total = _near_scores(total, after, before, rows)
    squares = _squares(panel) + _squares(after) + _squares(before) + _squares(far)
    return total + _dot_rows(rows[:, 2 * wide : 3 * wide], far), squares


def _pack(value):
    return (value * PACK).astype(jnp.float16)


def _unpack(value):
    return value.astype(jnp.float32) * (1.0 / PACK)


CHUNK = 128
FULL = lax.Precision.HIGHEST


def _chunks(count, body):
    def step(i, carry):
        body(pl.ds(pl.multiple_of(i * CHUNK, CHUNK), CHUNK))
        return carry

    lax.fori_loop(0, count // CHUNK, step, 0, unroll=True)


def _column_chunk(row_ref, cut, count):
    column = jnp.broadcast_to(row_ref[:, cut], (CHUNK, CHUNK)).T
    return jnp.concatenate([column] * (count // CHUNK), 1)


def _fold(value):
    return sum(value[:, i : i + CHUNK] for i in range(0, value.shape[1], CHUNK))


def _lane_sums(folded, copies):
    ones = jnp.ones((copies, CHUNK), jnp.float32)
    return lax.dot_general(
        ones, folded, (((1,), (1,)), ((), ())), precision=FULL, preferred_element_type=jnp.float32
    )


def _row_sums_kernel(target, weights_ref, column_ref, out_ref, scale_ref, total_ref):
    scale_ref[...] = target / jnp.sum(column_ref[...], 0)
    count, rows = weights_ref.shape
    total_ref[...] = jnp.zeros_like(total_ref)

    def body(cut):
        chunk = weights_ref[cut, :] * _column_chunk(scale_ref, cut, rows)
        total_ref[...] += jnp.sum(chunk.reshape(CHUNK // 8, 8, rows), 0)

    _chunks(count, body)
    total = jnp.sum(total_ref[...], 0, keepdims=True)
    out_ref[...] = jnp.broadcast_to(total[None], out_ref.shape)


def _column_sums_kernel(weights_ref, row_ref, out_ref, scale_ref):
    scale_ref[...] = 1.0 / jnp.sum(row_ref[...], 0)

    def body(cut):
        folded = _fold(weights_ref[cut, :] * scale_ref[...])
        out_ref[:, 0, cut] = _lane_sums(folded, out_ref.shape[0])

    _chunks(weights_ref.shape[0], body)


def _shares_kernel(
    target, weights_ref, column_ref, row_ref, shares_ref, mass_ref, column_scale_ref, row_scale_ref
):
    column_scale_ref[...] = target / jnp.sum(column_ref[...], 0)
    row_scale_ref[...] = 1.0 / jnp.sum(row_ref[...], 0)
    count, rows = weights_ref.shape

    def body(cut):
        scale = _column_chunk(column_scale_ref, cut, rows) * row_scale_ref[...]
        shares = (weights_ref[cut, :] * scale).astype(jnp.bfloat16)
        shares_ref[cut, :] = shares
        column_scale_ref[:, cut] = _lane_sums(_fold(shares.astype(jnp.float32)), 8)[:1]

    _chunks(count, body)
    mass_ref[...] = jnp.zeros_like(mass_ref)
    halves, _, width = mass_ref.shape
    for start in range(0, count, width):
        half, place = divmod(start, count // halves)
        mass_ref[half, place // width] = column_scale_ref[0, start : start + width]


def _whole(kernel, out_shape, scratch, *operands):
    inside = pl.BlockSpec(memory_space=pltpu.VMEM)
    return pl.pallas_call(
        kernel,
        out_shape=out_shape,
        in_specs=[inside] * len(operands),
        out_specs=jax.tree.map(lambda _: inside, out_shape),
        scratch_shapes=[pltpu.VMEM(shape, jnp.float32) for shape in scratch],
        compiler_params=pltpu.CompilerParams(vmem_limit_bytes=12 * 1024 * 1024),
    )(*operands)


def _copies(axis, count):
    return jax.ShapeDtypeStruct((lax.axis_size(axis), 1, count), jnp.float32)


def _exchange(copies, axis):
    return lax.all_to_all(copies, axis, 0, 0)


def _part_kernel(slots_ref, shares_ref, mass_ref, rows_ref, part_ref):
    count = shares_ref.shape[0]
    part_ref[0, :count] = jnp.dot(shares_ref[...], rows_ref[0], preferred_element_type=jnp.float32)
    part_ref[0, count:] = mass_ref[0]


def _part(shares, mass, halves, blocks, slots, flops=1000):
    count, rows = shares.shape[0] // 2, shares.shape[1]
    width = blocks.shape[2]
    extra = mass.shape[1]
    first, each = halves[0], slots[0].shape[0]
    return pl.pallas_call(
        _part_kernel,
        grid_spec=pltpu.PrefetchScalarGridSpec(
            num_scalar_prefetch=1,
            grid=(len(halves), each),
            in_specs=[
                pl.BlockSpec((count, rows), lambda h, i, slots: (first + h, 0)),
                pl.BlockSpec((1, extra, width), lambda h, i, slots: (first + h, 0, 0)),
                pl.BlockSpec((1, rows, width), lambda h, i, slots: (slots[h * each + i], 0, 0)),
            ],
            out_specs=pl.BlockSpec(
                (1, count + extra, width), lambda h, i, slots: (h * each + i, 0, 0)
            ),
        ),
        out_shape=jax.ShapeDtypeStruct((len(halves) * each, count + extra, width), jnp.float32),
        cost_estimate=pl.CostEstimate(flops=flops, bytes_accessed=flops // 512, transcendentals=0),
        compiler_params=pltpu.CompilerParams(vmem_limit_bytes=8 * 1024 * 1024),
    )(jnp.concatenate(slots), shares, mass, blocks)


def _ring_far(part, axis):
    low, high = part
    return _send(low, axis, 1), _send(high, axis, -1)


def _ring_near(after, before, far, axis):
    low, high = far
    spare = after.shape[0] // 2
    after = _pack(after + jnp.pad(_unpack(low), ((0, spare), (0, 0), (0, 0))))
    before = _pack(before + jnp.pad(_unpack(high), ((spare, 0), (0, 0), (0, 0))))
    return _send(after, axis, 1), _send(before, axis, -1)


def _scatter_sums(shares, mass, axes, blocks, slots):
    far, packed = [], []
    work = 2 * shares.shape[0] * shares.shape[1] * blocks.shape[2] * SIDE
    for half, (first, _) in enumerate(axes):
        part = _part(shares, mass, [half], blocks, [slots[half][0]], work)
        parts = _pack(part[: SIDE // 2]), _pack(part[SIDE // 2 :])
        packed.append(parts)
        far.append(_ring_far(parts, first))
    shares, packed = lax.optimization_barrier((shares, packed))
    near = [_part(shares, mass, [half], blocks, [slots[half][1]]) for half in range(2)]
    own = _part(shares, mass, [0, 1], blocks, [slot[2] for slot in slots])
    out = []
    for half, (first, second) in enumerate(axes):
        ends = _ring_near(near[half][:SIDE], near[half][SIDE:], far[half], first)
        line = [
            own[SIDE * half + i] + _unpack(ends[0][i]) + _unpack(ends[1][i]) for i in range(SIDE)
        ]
        came = [_send(_pack(line[i]), second, i) for i in (1, 3, 2)]
        out.append(line[0] + _unpack(came[0]) + _unpack(came[1]) + _unpack(came[2]))
    return out


def _place(place_ref, value, by_x_ref, by_z_ref):
    width = value.shape[1] // (SIDE * SIDE)
    for owner in range(SIDE * SIDE):
        off_x = lax.rem(owner // SIDE + SIDE - place_ref[0], SIDE)
        off_z = lax.rem(owner % SIDE + SIDE - place_ref[1], SIDE)
        block = value[:, owner * width : (owner + 1) * width]
        slot_x, slot_z = off_x * SIDE + off_z, off_z * SIDE + off_x
        for ref, slot in ((by_x_ref, slot_x), (by_z_ref, slot_z)):
            ref[:, pl.ds(pl.multiple_of(slot * width, width), width)] = block


def _reorder_kernel(place_ref, rows_ref, by_x_ref, by_z_ref, blocks_ref):
    rows = rows_ref[...]
    width = blocks_ref.shape[2]
    for i in range(SIDE * SIDE):
        blocks_ref[i] = rows[:, i * width : (i + 1) * width]
    rows = rows.astype(jnp.float32)
    inverse = lax.rsqrt(jnp.sum(rows * rows, 1, keepdims=True) + 1e-06)
    _place(place_ref, (rows * inverse).astype(jnp.bfloat16), by_x_ref, by_z_ref)


def _reorder(embeddings, place):
    rows, features = embeddings.shape
    tile = 128
    blocks = SIDE * SIDE
    width = features // blocks
    spec = pl.BlockSpec((tile, features), lambda i, place: (i, 0))
    shape = jax.ShapeDtypeStruct(embeddings.shape, jnp.bfloat16)
    by_x, by_z, split = pl.pallas_call(
        _reorder_kernel,
        grid_spec=pltpu.PrefetchScalarGridSpec(
            num_scalar_prefetch=1,
            grid=(rows // tile,),
            in_specs=[spec],
            out_specs=[
                spec,
                spec,
                pl.BlockSpec((blocks, tile, width), lambda i, place: (0, i, 0)),
            ],
        ),
        out_shape=[shape, shape, jax.ShapeDtypeStruct((blocks, rows, width), jnp.bfloat16)],
        cost_estimate=pl.CostEstimate(
            flops=3 * rows * features, bytes_accessed=8 * rows * features, transcendentals=rows
        ),
        compiler_params=pltpu.CompilerParams(vmem_limit_bytes=16 * 1024 * 1024),
    )(place, embeddings)
    return by_x, by_z, split


def on_device(embeddings, centroids):
    row_count = embeddings.shape[0]
    local_k = centroids.shape[0]
    half = local_k // 2
    me = lax.axis_index("dp")
    x, z = me // SIDE, me % SIDE
    offset = jnp.arange(SIDE, dtype=jnp.int32)
    along_x, along_z = lax.rem(x + offset, SIDE), lax.rem(z + offset, SIDE)
    grid = along_x[:, None] * SIDE + along_z[None, :]
    slots = [
        (table[2], jnp.concatenate([table[1], table[3]]), table[0]) for table in (grid, grid.T)
    ]
    place = jnp.stack([x, z]).astype(jnp.int32)
    panel_a = _line_panel(_z, centroids[:half])
    panel_b = _line_panel(_x, centroids[half:])
    place, slots, panel_a, panel_b = lax.optimization_barrier((place, slots, panel_a, panel_b))
    normed_x, normed_z, blocks = _reorder(embeddings, place)
    score_a, square_a = _gather_scores(_x, panel_a, normed_x)
    score_b, square_b = _gather_scores(_z, panel_b, normed_z)
    scores = jnp.concatenate([score_a, score_b], 0)
    scale = lax.rsqrt(jnp.concatenate([square_a, square_b]) + 1e-06)
    weights = jnp.exp(scores * scale[:, None] * 20.0)
    target = row_count * lax.axis_size("dp") / (local_k * lax.axis_size("cent"))
    column = jnp.broadcast_to(jnp.sum(weights, 1)[None, None], _copies("dp", local_k).shape)
    for sweep in range(ROUNDS):
        column = _exchange(column, "dp")
        row = _whole(
            functools.partial(_row_sums_kernel, target),
            _copies("cent", row_count),
            [(1, local_k), (8, row_count)],
            weights,
            column,
        )
        row = _exchange(row, "cent")
        if sweep + 1 < ROUNDS:
            column = _whole(
                _column_sums_kernel, _copies("dp", local_k), [(1, row_count)], weights, row
            )
    width = centroids.shape[1]
    shares, mass = _whole(
        functools.partial(_shares_kernel, target),
        (
            jax.ShapeDtypeStruct((local_k, row_count), jnp.bfloat16),
            jax.ShapeDtypeStruct((2, MASS_ROWS, width), jnp.float32),
        ),
        [(1, local_k), (1, row_count)],
        weights,
        column,
        row,
    )
    sums = _scatter_sums(shares, mass, [(_x, _z), (_z, _x)], blocks, slots)
    means = []
    for total in sums:
        mass = total[half:].reshape(-1)[:half]
        means.append((total[:half] / mass[:, None]).astype(jnp.bfloat16))
    first = lax.optimization_barrier(jnp.pad(means[0], ((0, half), (0, 0))))
    return (shares.T, lax.dynamic_update_slice(first, means[1], (half, 0)))


def solution(mesh):
    in_specs = (P("dp", None), P("cent", "dp"))
    out_specs = (P("dp", "cent"), P("cent", "dp"))
    return jax.shard_map(
        on_device, mesh=mesh, in_specs=in_specs, out_specs=out_specs, check_vma=False
    )
```

profile of v0, /device:TPU:0, one launch (start us, length us, event | category | flops | bytes accessed | tf_op | source)
XLA Modules:
  0.0 204.0 jit_solution(6769857907423905482)
XLA Ops:
  11.5 2.8 %collective-permute-start.7 = (bf16[256,256]{1,0:T(8,128)(2,1)S(1)}, bf16[256,256]{1,0:T(8,128)(2,1)S(1)}, u32[]{:S(2)}, u32[]{:S(2)}) collective-permute-start(bf16[256,256]{1,0:T(8,128)(2,1)S(1)} %slice.241), channel_id=1, source_target_pairs={{0,96},{8,104},{16,112},{24,120},{32,0},{40,8},{48,16},{56,24},{64... | collective-permute-start | bytes 393224 | tf_op jit(solution)/shard_map/ppermute | solution.py:29
  16.7 2.2 %collective-permute-start.3 = (bf16[256,256]{1,0:T(8,128)(2,1)S(1)}, bf16[256,256]{1,0:T(8,128)(2,1)S(1)}, u32[]{:S(2)}, u32[]{:S(2)}) collective-permute-start(bf16[256,256]{1,0:T(8,128)(2,1)S(1)} %slice.239), channel_id=1, source_target_pairs={{0,24},{8,0},{16,8},{24,16},{32,56},{40,32},{48,40},{56,48},{64,88... | collective-permute-start | bytes 393224 | tf_op jit(solution)/shard_map/ppermute | solution.py:29
  19.0 2.7 %collective-permute-done.2 = bf16[256,256]{1,0:T(8,128)(2,1)S(1)} collective-permute-done((bf16[256,256]{1,0:T(8,128)(2,1)S(1)}, bf16[256,256]{1,0:T(8,128)(2,1)S(1)}, u32[]{:S(2)}, u32[]{:S(2)}) %collective-permute-start.2) | collective-permute-done | bytes 131104 | tf_op jit(solution)/shard_map/ppermute | solution.py:29
  24.0 3.3 %collective-permute-start.12 = (bf16[512,1024]{1,0:T(8,128)(2,1)S(1)}, bf16[512,1024]{1,0:T(8,128)(2,1)S(1)}, u32[]{:S(2)}, u32[]{:S(2)}) collective-permute-start(bf16[512,1024]{1,0:T(8,128)(2,1)S(1)} %pad_maximum_fusion.1), channel_id=1, source_target_pairs={{0,24},{8,0},{16,8},{24,16},{32,56},{40,32},{48,40},{56,48},{64,88... | collective-permute-start | bytes 3145736 | tf_op jit(solution)/shard_map/ppermute | solution.py:29
  27.3 3.4 %copy-done.1 = bf16[1024,4096]{1,0:T(8,128)(2,1)S(1)} copy-done((bf16[1024,4096]{1,0:T(8,128)(2,1)S(1)}, bf16[1024,4096]{1,0:T(8,128)(2,1)}, u32[]{:S(2)}) %copy-start.1) | copy-done | bytes 8388632
  30.7 6.5 %shard_map.41 = (bf16[1024,4096]{1,0:T(8,128)(2,1)S(1)}, bf16[1024,4096]{1,0:T(8,128)(2,1)S(1)}, bf16[16,1024,256]{2,1,0:T(8,128)(2,1)S(1)}) custom-call(s32[2]{0:T(128)S(1)} %pad_add_fusion.place_ref, bf16[1024,4096]{1,0:T(8,128)(2,1)S(1)} %copy-done.1), custom_call_target="tpu_custom_call" | custom-call | flops 12582912 | bytes 33554432 | tf_op jit(solution)/shard_map/pallas_call | solution.py:292
  40.4 6.3 %collective-permute-done.9.before_ref = bf16[512,1024]{1,0:T(8,128)(2,1)S(1)} collective-permute-done((bf16[512,1024]{1,0:T(8,128)(2,1)S(1)}, bf16[512,1024]{1,0:T(8,128)(2,1)S(1)}, u32[]{:S(2)}, u32[]{:S(2)}) %collective-permute-start.9) | collective-permute-done | bytes 1048608 | tf_op jit(solution)/shard_map/ppermute | solution.py:29
  46.8 3.3 %collective-permute-start.11 = (bf16[256,1024]{1,0:T(8,128)(2,1)S(1)}, bf16[256,1024]{1,0:T(8,128)(2,1)S(1)}, u32[]{:S(2)}, u32[]{:S(2)}) collective-permute-start(bf16[256,1024]{1,0:T(8,128)(2,1)S(1)} %slice.243), channel_id=1, source_target_pairs={{0,96},{8,104},{16,112},{24,120},{32,0},{40,8},{48,16},{56,24},{64... | collective-permute-start | bytes 1572872 | tf_op jit(solution)/shard_map/ppermute | solution.py:29
  51.1 2.7 %collective-permute-start.15 = (bf16[256,1024]{1,0:T(8,128)(2,1)S(1)}, bf16[256,1024]{1,0:T(8,128)(2,1)S(1)}, u32[]{:S(2)}, u32[]{:S(2)}) collective-permute-start(bf16[256,1024]{1,0:T(8,128)(2,1)S(1)} %slice.245), channel_id=1, source_target_pairs={{0,24},{8,0},{16,8},{24,16},{32,56},{40,32},{48,40},{56,48},{64,88... | collective-permute-start | bytes 1572872 | tf_op jit(solution)/shard_map/ppermute | solution.py:29
  54.3 3.6 %shard_map.42 = f32[512,1024]{1,0:T(8,128)S(1)} custom-call(f32[512,1024]{1,0:T(8,128)S(1)} %fusion.16.total_ref, bf16[512,1024]{1,0:T(8,128)(2,1)S(1)} %collective-permute-done.8.after_ref, bf16[512,1024]{1,0:T(8,128)(2,1)S(1)} %collective-permute-done.9.before_ref, bf16[1024,4096]{1,0:T(8,128)(2,1)S(1)} %get-tuple-element.19.rows_1_ref.rows_3_ref, ...), custom_call_target="tpu_custom_call" | custom-call | flops 2147483648 | bytes 10485760 | tf_op jit(solution)/shard_map/pallas_call | solution.py:67
  58.5 3.6 %shard_map.43 = f32[512,1024]{1,0:T(8,128)S(1)} custom-call(f32[512,1024]{1,0:T(8,128)S(1)} %fusion.12.total_ref, bf16[512,1024]{1,0:T(8,128)(2,1)S(1)} %collective-permute-done.12.after_ref, bf16[512,1024]{1,0:T(8,128)(2,1)S(1)} %collective-permute-done.13.before_ref, bf16[1024,4096]{1,0:T(8,128)(2,1)S(1)} %get-tuple-element.21.rows_1_ref.rows_3_ref, ...), custom_call_target="tpu_custom_call" | custom-call | flops 2147483648 | bytes 10485760 | tf_op jit(solution)/shard_map/pallas_call | solution.py:67
  67.4 11.4 %all_to_all.30.column_ref = f32[16,1,1024]{2,1,0:T(1,128)S(1)} all-to-all(f32[16,1,1024]{2,1,0:T(1,128)S(1)} %broadcast_in_dim.2), channel_id=1, replica_groups=mesh['dp'=16,'cent'=8] {'dp'}, dimensions={0} | all-to-all | bytes 131072 | tf_op jit(solution)/shard_map/all_to_all | solution.py:195
  79.2 9.7 %all_to_all.31.row_ref = f32[8,1,1024]{2,1,0:T(1,128)S(1)} all-to-all(f32[8,1,1024]{2,1,0:T(1,128)S(1)} %shard_map.44), channel_id=1, replica_groups=mesh['dp'=16,'cent'=8] {'cent'}, dimensions={0} | all-to-all | bytes 65536 | tf_op jit(solution)/shard_map/all_to_all | solution.py:195
  90.0 10.9 %all_to_all.32.column_ref = f32[16,1,1024]{2,1,0:T(1,128)S(1)} all-to-all(f32[16,1,1024]{2,1,0:T(1,128)S(1)} %shard_map.45), channel_id=1, replica_groups=mesh['dp'=16,'cent'=8] {'dp'}, dimensions={0} | all-to-all | bytes 131072 | tf_op jit(solution)/shard_map/all_to_all | solution.py:195
  101.3 7.8 %all_to_all.33.row_ref = f32[8,1,1024]{2,1,0:T(1,128)S(1)} all-to-all(f32[8,1,1024]{2,1,0:T(1,128)S(1)} %shard_map.46), channel_id=1, replica_groups=mesh['dp'=16,'cent'=8] {'cent'}, dimensions={0} | all-to-all | bytes 65536 | tf_op jit(solution)/shard_map/all_to_all | solution.py:195
  110.1 10.9 %all_to_all.34.column_ref = f32[16,1,1024]{2,1,0:T(1,128)S(1)} all-to-all(f32[16,1,1024]{2,1,0:T(1,128)S(1)} %shard_map.47), channel_id=1, replica_groups=mesh['dp'=16,'cent'=8] {'dp'}, dimensions={0} | all-to-all | bytes 131072 | tf_op jit(solution)/shard_map/all_to_all | solution.py:195
  121.4 7.8 %all_to_all.35.row_ref = f32[8,1,1024]{2,1,0:T(1,128)S(1)} all-to-all(f32[8,1,1024]{2,1,0:T(1,128)S(1)} %shard_map.48), channel_id=1, replica_groups=mesh['dp'=16,'cent'=8] {'cent'}, dimensions={0} | all-to-all | bytes 65536 | tf_op jit(solution)/shard_map/all_to_all | solution.py:195
  130.7 2.4 %shard_map.50 = f32[4,528,256]{2,1,0:T(8,128)S(1)} custom-call(s32[4]{0:T(128)S(1)} %get-tuple-element.25.slots_ref, bf16[1024,1024]{1,0:T(8,128)(2,1)S(1)} %get-tuple-element.29.shares_ref, f32[2,16,256]{2,1,0:T(8,128)S(1)} %get-tuple-element.26.mass_ref, bf16[16,1024,256]{2,1,0:T(8,128)(2,1)S(1)} %get-tuple-element.27.rows_ref), custom_call_target="tpu_custom_call" | custom-call | flops 2147483648 | bytes 4194304 | tf_op jit(solution)/shard_map/pallas_call | solution.py:209
  135.5 2.4 %shard_map.51 = f32[4,528,256]{2,1,0:T(8,128)S(1)} custom-call(s32[4]{0:T(128)S(1)} %get-tuple-element.28.slots_ref, bf16[1024,1024]{1,0:T(8,128)(2,1)S(1)} %get-tuple-element.29.shares_ref, f32[2,16,256]{2,1,0:T(8,128)S(1)} %get-tuple-element.26.mass_ref, bf16[16,1024,256]{2,1,0:T(8,128)(2,1)S(1)} %get-tuple-element.27.rows_ref), custom_call_target="tpu_custom_call" | custom-call | flops 2147483648 | bytes 4194304 | tf_op jit(solution)/shard_map/pallas_call | solution.py:209
  140.2 4.2 %shard_map.53 = f32[8,528,256]{2,1,0:T(8,128)S(1)} custom-call(s32[8]{0:T(128)S(1)} %pad_add_fusion.1.slots_ref, bf16[1024,1024]{1,0:T(8,128)(2,1)S(1)} %get-tuple-element.29.shares_ref, f32[2,16,256]{2,1,0:T(8,128)S(1)} %get-tuple-element.26.mass_ref, bf16[16,1024,256]{2,1,0:T(8,128)(2,1)S(1)} %get-tuple-element.27.rows_ref), custom_call_target="tpu_custom_call" | custom-call | flops 1000 | bytes 1 | tf_op jit(solution)/shard_map/pallas_call | solution.py:209
  144.4 4.2 %shard_map.54 = f32[8,528,256]{2,1,0:T(8,128)S(1)} custom-call(s32[8]{0:T(128)S(1)} %pad_add_fusion.2.slots_ref, bf16[1024,1024]{1,0:T(8,128)(2,1)S(1)} %get-tuple-element.29.shares_ref, f32[2,16,256]{2,1,0:T(8,128)S(1)} %get-tuple-element.26.mass_ref, bf16[16,1024,256]{2,1,0:T(8,128)(2,1)S(1)} %get-tuple-element.27.rows_ref), custom_call_target="tpu_custom_call" | custom-call | flops 1000 | bytes 1 | tf_op jit(solution)/shard_map/pallas_call | solution.py:209
  150.3 3.2 %collective-permute-start.19 = (f16[4,528,256]{2,1,0:T(8,128)(2,1)S(1)}, f16[4,528,256]{2,1,0:T(8,128)(2,1)S(1)}, u32[]{:S(2)}, u32[]{:S(2)}) collective-permute-start(f16[4,528,256]{2,1,0:T(8,128)(2,1)S(1)} %get-tuple-element.50), channel_id=1, source_target_pairs={{0,96},{8,104},{16,112},{24,120},{32,0},{40,8},{48,16},{56,24},{64... | collective-permute-start | bytes 3244040 | tf_op jit(solution)/shard_map/ppermute | solution.py:29
  155.1 2.8 %collective-permute-start.26 = (f16[4,528,256]{2,1,0:T(8,128)(2,1)S(1)}, f16[4,528,256]{2,1,0:T(8,128)(2,1)S(1)}, u32[]{:S(2)}, u32[]{:S(2)}) collective-permute-start(f16[4,528,256]{2,1,0:T(8,128)(2,1)S(1)} %get-tuple-element.48), channel_id=1, source_target_pairs={{0,24},{8,0},{16,8},{24,16},{32,56},{40,32},{48,40},{56,48},{64,88... | collective-permute-start | bytes 3244040 | tf_op jit(solution)/shard_map/ppermute | solution.py:29
  157.9 4.2 %shard_map.52 = f32[8,528,256]{2,1,0:T(8,128)S(1)} custom-call(s32[8]{0:T(128)S(1)} %pad_add_fusion.3.slots_ref, bf16[1024,1024]{1,0:T(8,128)(2,1)S(1)} %get-tuple-element.29.shares_ref, f32[2,16,256]{2,1,0:T(8,128)S(1)} %get-tuple-element.26.mass_ref, bf16[16,1024,256]{2,1,0:T(8,128)(2,1)S(1)} %get-tuple-element.27.rows_ref), custom_call_target="tpu_custom_call" | custom-call | flops 1000 | bytes 1 | tf_op jit(solution)/shard_map/pallas_call | solution.py:209
  162.2 13.7 %collective-permute-done.17 = f16[4,528,256]{2,1,0:T(8,128)(2,1)S(1)} collective-permute-done((f16[4,528,256]{2,1,0:T(8,128)(2,1)S(1)}, f16[4,528,256]{2,1,0:T(8,128)(2,1)S(1)}, u32[]{:S(2)}, u32[]{:S(2)}) %collective-permute-start.17) | collective-permute-done | bytes 1081376 | tf_op jit(solution)/shard_map/ppermute | solution.py:29
  175.9 3.7 %collective-permute-done.24 = f16[4,528,256]{2,1,0:T(8,128)(2,1)S(1)} collective-permute-done((f16[4,528,256]{2,1,0:T(8,128)(2,1)S(1)}, f16[4,528,256]{2,1,0:T(8,128)(2,1)S(1)}, u32[]{:S(2)}, u32[]{:S(2)}) %collective-permute-start.24) | collective-permute-done | bytes 1081376 | tf_op jit(solution)/shard_map/ppermute | solution.py:29
  181.7 3.2 %collective-permute-start.21 = (f16[528,256]{1,0:T(8,128)(2,1)}, f16[528,256]{1,0:T(8,128)(2,1)}, u32[]{:S(2)}, u32[]{:S(2)}) collective-permute-start(f16[528,256]{1,0:T(8,128)(2,1)} %get-tuple-element.44), channel_id=1, source_target_pairs={{0,24},{8,0},{16,8},{24,16},{32,56},{40,32},{48,40},{56,48},{64,88... | collective-permute-start | bytes 811016 | tf_op jit(solution)/shard_map/ppermute | solution.py:29
  186.6 2.8 %collective-permute-start.28 = (f16[528,256]{1,0:T(8,128)(2,1)}, f16[528,256]{1,0:T(8,128)(2,1)}, u32[]{:S(2)}, u32[]{:S(2)}) collective-permute-start(f16[528,256]{1,0:T(8,128)(2,1)} %get-tuple-element.38), channel_id=1, source_target_pairs={{0,96},{8,104},{16,112},{24,120},{32,0},{40,8},{48,16},{56,24},{64... | collective-permute-start | bytes 811016 | tf_op jit(solution)/shard_map/ppermute | solution.py:29
  189.3 2.8 %collective-permute-done.20 = f16[528,256]{1,0:T(8,128)(2,1)S(1)} collective-permute-done((f16[528,256]{1,0:T(8,128)(2,1)S(1)}, f16[528,256]{1,0:T(8,128)(2,1)S(1)}, u32[]{:S(2)}, u32[]{:S(2)}) %collective-permute-start.20) | collective-permute-done | bytes 270368 | tf_op jit(solution)/shard_map/ppermute | solution.py:29
  193.3 2.5 %copy.4 = bf16[1024,1024]{1,0:T(8,128)(2,1)} copy(bf16[1024,1024]{0,1:T(8,128)(2,1)S(1)} %bitcast.57) | data formatting | bytes 4194304
  195.9 4.5 %collective-permute-done.29 = f16[528,256]{1,0:T(8,128)(2,1)} collective-permute-done((f16[528,256]{1,0:T(8,128)(2,1)}, f16[528,256]{1,0:T(8,128)(2,1)}, u32[]{:S(2)}, u32[]{:S(2)}) %collective-permute-start.29) | collective-permute-done | bytes 270368 | tf_op jit(solution)/shard_map/ppermute | solution.py:29
  200.4 2.4 %fusion.35 = (f32[528,256]{1,0:T(8,128)S(1)}, f32[528,256]{1,0:T(8,128)S(1)}) fusion(f32[8,528,256]{2,1,0:T(8,128)} %copy-done, f16[528,256]{1,0:T(8,128)(2,1)} %collective-permute-done.29, f16[528,256]{1,0:T(8,128)(2,1)} %collective-permute-done.28, f16[528,256]{1,0:T(8,128)(2,1)} %collective-permute-done.27, f16[4,528,256]{2,1,0:T(8,128)(2,1)} %copy-done.4, ...), kind=kLoop, calls=%fused_computation.62 | loop fusion | flops 4055040 | bytes 4866048 | tf_op jit(solution)/shard_map/add | solution.py:260
  (120 shorter events, 44.7 us)
Async XLA Ops:
  1.7 9.2 %collective-permute-start.5 = (bf16[512,256]{1,0:T(8,128)(2,1)S(1)}, bf16[512,256]{1,0:T(8,128)(2,1)S(1)}, u32[]{:S(2)}, u32[]{:S(2)}) collective-permute-start(bf16[512,256]{1,0:T(8,128)(2,1)S(1)} %get-tuple-element.55), channel_id=1, source_target_pairs={{0,32},{8,40},{16,48},{24,56},{32,64},{40,72},{48,80},{56,88},{64,... | collective-permute-start | bytes 786440 | tf_op jit(solution)/shard_map/ppermute | solution.py:29
  3.3 8.1 %collective-permute-start.4 = (bf16[512,256]{1,0:T(8,128)(2,1)S(1)}, bf16[512,256]{1,0:T(8,128)(2,1)S(1)}, u32[]{:S(2)}, u32[]{:S(2)}) collective-permute-start(bf16[512,256]{1,0:T(8,128)(2,1)S(1)} %get-tuple-element.55), channel_id=1, source_target_pairs={{0,96},{8,104},{16,112},{24,120},{32,0},{40,8},{48,16},{56,24},{64... | collective-permute-start | bytes 786440 | tf_op jit(solution)/shard_map/ppermute | solution.py:29
  5.0 9.9 %collective-permute-start.1 = (bf16[512,256]{1,0:T(8,128)(2,1)S(1)}, bf16[512,256]{1,0:T(8,128)(2,1)S(1)}, u32[]{:S(2)}, u32[]{:S(2)}) collective-permute-start(bf16[512,256]{1,0:T(8,128)(2,1)S(1)} %get-tuple-element.56), channel_id=1, source_target_pairs={{0,8},{8,16},{16,24},{24,0},{32,40},{40,48},{48,56},{56,32},{64,72... | collective-permute-start | bytes 786440 | tf_op jit(solution)/shard_map/ppermute | solution.py:29
  7.0 9.7 %collective-permute-start = (bf16[512,256]{1,0:T(8,128)(2,1)S(1)}, bf16[512,256]{1,0:T(8,128)(2,1)S(1)}, u32[]{:S(2)}, u32[]{:S(2)}) collective-permute-start(bf16[512,256]{1,0:T(8,128)(2,1)S(1)} %get-tuple-element.56), channel_id=1, source_target_pairs={{0,24},{8,0},{16,8},{24,16},{32,56},{40,32},{48,40},{56,48},{64,88... | collective-permute-start | bytes 786440 | tf_op jit(solution)/shard_map/ppermute | solution.py:29
  10.9 8.0 %collective-permute-start.6 = (bf16[256,256]{1,0:T(8,128)(2,1)S(1)}, bf16[256,256]{1,0:T(8,128)(2,1)S(1)}, u32[]{:S(2)}, u32[]{:S(2)}) collective-permute-start(bf16[256,256]{1,0:T(8,128)(2,1)S(1)} %slice.240), channel_id=1, source_target_pairs={{0,32},{8,40},{16,48},{24,56},{32,64},{40,72},{48,80},{56,88},{64,... | collective-permute-start | bytes 393224 | tf_op jit(solution)/shard_map/ppermute | solution.py:29
  11.5 7.4 %collective-permute-start.7 = (bf16[256,256]{1,0:T(8,128)(2,1)S(1)}, bf16[256,256]{1,0:T(8,128)(2,1)S(1)}, u32[]{:S(2)}, u32[]{:S(2)}) collective-permute-start(bf16[256,256]{1,0:T(8,128)(2,1)S(1)} %slice.241), channel_id=1, source_target_pairs={{0,96},{8,104},{16,112},{24,120},{32,0},{40,8},{48,16},{56,24},{64... | collective-permute-start | bytes 393224 | tf_op jit(solution)/shard_map/ppermute | solution.py:29
  14.9 6.9 %collective-permute-start.2 = (bf16[256,256]{1,0:T(8,128)(2,1)S(1)}, bf16[256,256]{1,0:T(8,128)(2,1)S(1)}, u32[]{:S(2)}, u32[]{:S(2)}) collective-permute-start(bf16[256,256]{1,0:T(8,128)(2,1)S(1)} %slice.238), channel_id=1, source_target_pairs={{0,8},{8,16},{16,24},{24,0},{32,40},{40,48},{48,56},{56,32},{64,72... | collective-permute-start | bytes 393224 | tf_op jit(solution)/shard_map/ppermute | solution.py:29
  16.7 5.1 %collective-permute-start.3 = (bf16[256,256]{1,0:T(8,128)(2,1)S(1)}, bf16[256,256]{1,0:T(8,128)(2,1)S(1)}, u32[]{:S(2)}, u32[]{:S(2)}) collective-permute-start(bf16[256,256]{1,0:T(8,128)(2,1)S(1)} %slice.239), channel_id=1, source_target_pairs={{0,24},{8,0},{16,8},{24,16},{32,56},{40,32},{48,40},{56,48},{64,88... | collective-permute-start | bytes 393224 | tf_op jit(solution)/shard_map/ppermute | solution.py:29
  21.9 24.9 %collective-permute-start.8 = (bf16[512,1024]{1,0:T(8,128)(2,1)S(1)}, bf16[512,1024]{1,0:T(8,128)(2,1)S(1)}, u32[]{:S(2)}, u32[]{:S(2)}) collective-permute-start(bf16[512,1024]{1,0:T(8,128)(2,1)S(1)} %pad_maximum_fusion), channel_id=1, source_target_pairs={{0,96},{8,104},{16,112},{24,120},{32,0},{40,8},{48,16},{56,24},{64... | collective-permute-start | bytes 3145736 | tf_op jit(solution)/shard_map/ppermute | solution.py:29
  22.9 23.8 %collective-permute-start.9 = (bf16[512,1024]{1,0:T(8,128)(2,1)S(1)}, bf16[512,1024]{1,0:T(8,128)(2,1)S(1)}, u32[]{:S(2)}, u32[]{:S(2)}) collective-permute-start(bf16[512,1024]{1,0:T(8,128)(2,1)S(1)} %pad_maximum_fusion), channel_id=1, source_target_pairs={{0,32},{8,40},{16,48},{24,56},{32,64},{40,72},{48,80},{56,88},{64,... | collective-permute-start | bytes 3145736 | tf_op jit(solution)/shard_map/ppermute | solution.py:29
  24.0 27.1 %collective-permute-start.12 = (bf16[512,1024]{1,0:T(8,128)(2,1)S(1)}, bf16[512,1024]{1,0:T(8,128)(2,1)S(1)}, u32[]{:S(2)}, u32[]{:S(2)}) collective-permute-start(bf16[512,1024]{1,0:T(8,128)(2,1)S(1)} %pad_maximum_fusion.1), channel_id=1, source_target_pairs={{0,24},{8,0},{16,8},{24,16},{32,56},{40,32},{48,40},{56,48},{64,88... | collective-permute-start | bytes 3145736 | tf_op jit(solution)/shard_map/ppermute | solution.py:29
  27.3 22.8 %collective-permute-start.13 = (bf16[512,1024]{1,0:T(8,128)(2,1)S(1)}, bf16[512,1024]{1,0:T(8,128)(2,1)S(1)}, u32[]{:S(2)}, u32[]{:S(2)}) collective-permute-start(bf16[512,1024]{1,0:T(8,128)(2,1)S(1)} %pad_maximum_fusion.1), channel_id=1, source_target_pairs={{0,8},{8,16},{16,24},{24,0},{32,40},{40,48},{48,56},{56,32},{64,72... | collective-permute-start | bytes 3145736 | tf_op jit(solution)/shard_map/ppermute | solution.py:29
  46.7 15.4 %collective-permute-start.10 = (bf16[256,1024]{1,0:T(8,128)(2,1)S(1)}, bf16[256,1024]{1,0:T(8,128)(2,1)S(1)}, u32[]{:S(2)}, u32[]{:S(2)}) collective-permute-start(bf16[256,1024]{1,0:T(8,128)(2,1)S(1)} %slice.242), channel_id=1, source_target_pairs={{0,32},{8,40},{16,48},{24,56},{32,64},{40,72},{48,80},{56,88},{64,... | collective-permute-start | bytes 1572872 | tf_op jit(solution)/shard_map/ppermute | solution.py:29
  46.8 15.4 %collective-permute-start.11 = (bf16[256,1024]{1,0:T(8,128)(2,1)S(1)}, bf16[256,1024]{1,0:T(8,128)(2,1)S(1)}, u32[]{:S(2)}, u32[]{:S(2)}) collective-permute-start(bf16[256,1024]{1,0:T(8,128)(2,1)S(1)} %slice.243), channel_id=1, source_target_pairs={{0,96},{8,104},{16,112},{24,120},{32,0},{40,8},{48,16},{56,24},{64... | collective-permute-start | bytes 1572872 | tf_op jit(solution)/shard_map/ppermute | solution.py:29
  50.2 12.0 %collective-permute-start.14 = (bf16[256,1024]{1,0:T(8,128)(2,1)S(1)}, bf16[256,1024]{1,0:T(8,128)(2,1)S(1)}, u32[]{:S(2)}, u32[]{:S(2)}) collective-permute-start(bf16[256,1024]{1,0:T(8,128)(2,1)S(1)} %slice.244), channel_id=1, source_target_pairs={{0,8},{8,16},{16,24},{24,0},{32,40},{40,48},{48,56},{56,32},{64,72... | collective-permute-start | bytes 1572872 | tf_op jit(solution)/shard_map/ppermute | solution.py:29
  51.1 12.8 %collective-permute-start.15 = (bf16[256,1024]{1,0:T(8,128)(2,1)S(1)}, bf16[256,1024]{1,0:T(8,128)(2,1)S(1)}, u32[]{:S(2)}, u32[]{:S(2)}) collective-permute-start(bf16[256,1024]{1,0:T(8,128)(2,1)S(1)} %slice.245), channel_id=1, source_target_pairs={{0,24},{8,0},{16,8},{24,16},{32,56},{40,32},{48,40},{56,48},{64,88... | collective-permute-start | bytes 1572872 | tf_op jit(solution)/shard_map/ppermute | solution.py:29
  133.4 15.3 %collective-permute-start.18 = (f16[2,528,256]{2,1,0:T(8,128)(2,1)S(1)}, f16[2,528,256]{2,1,0:T(8,128)(2,1)S(1)}, u32[]{:S(2)}, u32[]{:S(2)}) collective-permute-start(f16[2,528,256]{2,1,0:T(8,128)(2,1)S(1)} %get-tuple-element.53), channel_id=1, source_target_pairs={{0,96},{8,104},{16,112},{24,120},{32,0},{40,8},{48,16},{56,24},{64... | collective-permute-start | bytes 1622024 | tf_op jit(solution)/shard_map/ppermute | solution.py:29
  134.6 14.9 %collective-permute-start.16 = (f16[2,528,256]{2,1,0:T(8,128)(2,1)S(1)}, f16[2,528,256]{2,1,0:T(8,128)(2,1)S(1)}, u32[]{:S(2)}, u32[]{:S(2)}) collective-permute-start(f16[2,528,256]{2,1,0:T(8,128)(2,1)S(1)} %get-tuple-element.54), channel_id=1, source_target_pairs={{0,32},{8,40},{16,48},{24,56},{32,64},{40,72},{48,80},{56,88},{64,... | collective-permute-start | bytes 1622024 | tf_op jit(solution)/shard_map/ppermute | solution.py:29
  138.1 15.5 %collective-permute-start.25 = (f16[2,528,256]{2,1,0:T(8,128)(2,1)S(1)}, f16[2,528,256]{2,1,0:T(8,128)(2,1)S(1)}, u32[]{:S(2)}, u32[]{:S(2)}) collective-permute-start(f16[2,528,256]{2,1,0:T(8,128)(2,1)S(1)} %get-tuple-element.51), channel_id=1, source_target_pairs={{0,24},{8,0},{16,8},{24,16},{32,56},{40,32},{48,40},{56,48},{64,88... | collective-permute-start | bytes 1622024 | tf_op jit(solution)/shard_map/ppermute | solution.py:29
  139.4 14.3 %collective-permute-start.23 = (f16[2,528,256]{2,1,0:T(8,128)(2,1)S(1)}, f16[2,528,256]{2,1,0:T(8,128)(2,1)S(1)}, u32[]{:S(2)}, u32[]{:S(2)}) collective-permute-start(f16[2,528,256]{2,1,0:T(8,128)(2,1)S(1)} %get-tuple-element.52), channel_id=1, source_target_pairs={{0,8},{8,16},{16,24},{24,0},{32,40},{40,48},{48,56},{56,32},{64,72... | collective-permute-start | bytes 1622024 | tf_op jit(solution)/shard_map/ppermute | solution.py:29
  150.2 25.6 %collective-permute-start.17 = (f16[4,528,256]{2,1,0:T(8,128)(2,1)S(1)}, f16[4,528,256]{2,1,0:T(8,128)(2,1)S(1)}, u32[]{:S(2)}, u32[]{:S(2)}) collective-permute-start(f16[4,528,256]{2,1,0:T(8,128)(2,1)S(1)} %get-tuple-element.49), channel_id=1, source_target_pairs={{0,32},{8,40},{16,48},{24,56},{32,64},{40,72},{48,80},{56,88},{64,... | collective-permute-start | bytes 3244040 | tf_op jit(solution)/shard_map/ppermute | solution.py:29
  150.3 25.5 %collective-permute-start.19 = (f16[4,528,256]{2,1,0:T(8,128)(2,1)S(1)}, f16[4,528,256]{2,1,0:T(8,128)(2,1)S(1)}, u32[]{:S(2)}, u32[]{:S(2)}) collective-permute-start(f16[4,528,256]{2,1,0:T(8,128)(2,1)S(1)} %get-tuple-element.50), channel_id=1, source_target_pairs={{0,96},{8,104},{16,112},{24,120},{32,0},{40,8},{48,16},{56,24},{64... | collective-permute-start | bytes 3244040 | tf_op jit(solution)/shard_map/ppermute | solution.py:29
  154.6 25.1 %collective-permute-start.24 = (f16[4,528,256]{2,1,0:T(8,128)(2,1)S(1)}, f16[4,528,256]{2,1,0:T(8,128)(2,1)S(1)}, u32[]{:S(2)}, u32[]{:S(2)}) collective-permute-start(f16[4,528,256]{2,1,0:T(8,128)(2,1)S(1)} %get-tuple-element.47), channel_id=1, source_target_pairs={{0,8},{8,16},{16,24},{24,0},{32,40},{40,48},{48,56},{56,32},{64,72... | collective-permute-start | bytes 3244040 | tf_op jit(solution)/shard_map/ppermute | solution.py:29
  155.1 24.5 %collective-permute-start.26 = (f16[4,528,256]{2,1,0:T(8,128)(2,1)S(1)}, f16[4,528,256]{2,1,0:T(8,128)(2,1)S(1)}, u32[]{:S(2)}, u32[]{:S(2)}) collective-permute-start(f16[4,528,256]{2,1,0:T(8,128)(2,1)S(1)} %get-tuple-element.48), channel_id=1, source_target_pairs={{0,24},{8,0},{16,8},{24,16},{32,56},{40,32},{48,40},{56,48},{64,88... | collective-permute-start | bytes 3244040 | tf_op jit(solution)/shard_map/ppermute | solution.py:29
  162.2 19.4 %copy-start = (f32[8,528,256]{2,1,0:T(8,128)}, f32[8,528,256]{2,1,0:T(8,128)S(1)}, u32[]{:S(2)}) copy-start(f32[8,528,256]{2,1,0:T(8,128)S(1)} %shard_map.52) | copy-start | bytes 12976132
  175.9 5.7 %copy-start.2 = (f16[4,528,256]{2,1,0:T(8,128)(2,1)}, f16[4,528,256]{2,1,0:T(8,128)(2,1)S(1)}, u32[]{:S(2)}) copy-start(f16[4,528,256]{2,1,0:T(8,128)(2,1)S(1)} %collective-permute-done.19) | copy-start | bytes 3244036
  181.6 10.5 %collective-permute-start.20 = (f16[528,256]{1,0:T(8,128)(2,1)S(1)}, f16[528,256]{1,0:T(8,128)(2,1)S(1)}, u32[]{:S(2)}, u32[]{:S(2)}) collective-permute-start(f16[528,256]{1,0:T(8,128)(2,1)S(1)} %get-tuple-element.46), channel_id=1, source_target_pairs={{0,8},{8,16},{16,24},{24,0},{32,40},{40,48},{48,56},{56,32},{64,72... | collective-permute-start | bytes 811016 | tf_op jit(solution)/shard_map/ppermute | solution.py:29
  181.7 14.2 %collective-permute-start.21 = (f16[528,256]{1,0:T(8,128)(2,1)}, f16[528,256]{1,0:T(8,128)(2,1)}, u32[]{:S(2)}, u32[]{:S(2)}) collective-permute-start(f16[528,256]{1,0:T(8,128)(2,1)} %get-tuple-element.44), channel_id=1, source_target_pairs={{0,24},{8,0},{16,8},{24,16},{32,56},{40,32},{48,40},{56,48},{64,88... | collective-permute-start | bytes 811016 | tf_op jit(solution)/shard_map/ppermute | solution.py:29
  184.9 11.0 %collective-permute-start.22 = (f16[528,256]{1,0:T(8,128)(2,1)}, f16[528,256]{1,0:T(8,128)(2,1)}, u32[]{:S(2)}, u32[]{:S(2)}) collective-permute-start(f16[528,256]{1,0:T(8,128)(2,1)} %get-tuple-element.45), channel_id=1, source_target_pairs={{0,16},{8,24},{16,0},{24,8},{32,48},{40,56},{48,32},{56,40},{64,80... | collective-permute-start | bytes 811016 | tf_op jit(solution)/shard_map/ppermute | solution.py:29
  186.1 9.8 %collective-permute-start.27 = (f16[528,256]{1,0:T(8,128)(2,1)}, f16[528,256]{1,0:T(8,128)(2,1)}, u32[]{:S(2)}, u32[]{:S(2)}) collective-permute-start(f16[528,256]{1,0:T(8,128)(2,1)} %get-tuple-element.36), channel_id=1, source_target_pairs={{0,32},{8,40},{16,48},{24,56},{32,64},{40,72},{48,80},{56,88},{64,... | collective-permute-start | bytes 811016 | tf_op jit(solution)/shard_map/ppermute | solution.py:29
  186.6 9.3 %collective-permute-start.28 = (f16[528,256]{1,0:T(8,128)(2,1)}, f16[528,256]{1,0:T(8,128)(2,1)}, u32[]{:S(2)}, u32[]{:S(2)}) collective-permute-start(f16[528,256]{1,0:T(8,128)(2,1)} %get-tuple-element.38), channel_id=1, source_target_pairs={{0,96},{8,104},{16,112},{24,120},{32,0},{40,8},{48,16},{56,24},{64... | collective-permute-start | bytes 811016 | tf_op jit(solution)/shard_map/ppermute | solution.py:29
  192.1 8.3 %collective-permute-start.29 = (f16[528,256]{1,0:T(8,128)(2,1)}, f16[528,256]{1,0:T(8,128)(2,1)}, u32[]{:S(2)}, u32[]{:S(2)}) collective-permute-start(f16[528,256]{1,0:T(8,128)(2,1)} %get-tuple-element.37), channel_id=1, source_target_pairs={{0,64},{8,72},{16,80},{24,88},{32,96},{40,104},{48,112},{56,120},{... | collective-permute-start | bytes 811016 | tf_op jit(solution)/shard_map/ppermute | solution.py:29
  (4 other events, 8.1 us)
where the time goes:
time: 204 us
  blocking collectives  58.5 us (29%)
  starting transfers between devices  46.8 us (23%)
  waiting for transfers between devices  36.6 us (18%)
  Pallas kernels  35.9 us (18%)
  other arithmetic  11.7 us (6%)
  local copies, waits for them, and re-layouts  8.2 us (4%)
  matrix products  5.15 us (3%)
    all_to_all x6, blocking collectives, _exchange(): return lax.all_to_all(copies, axis, 0, 0)  58.5 us
    ppermute x30, starting transfers between devices, _send(): return lax.ppermute(value, 'dp', axis(step))  46.8 us
    ppermute x30, waiting for transfers between devices, _send(): return lax.ppermute(value, 'dp', axis(step))  36.6 us
    pallas_call x5, Pallas kernels, _part(): pl.pallas_call(_part_kernel, grid_spec=pltpu.PrefetchScalarGridSpec(num_s...  17.5 us
    pallas_call x2, Pallas kernels, _near_scores(): pl.pallas_call(_near_scores_kernel, grid=(SIDE,), in_specs=[tiles, panel,...  7.19 us
    unnamed x19, local copies, waits for them, and re-layouts  6.8 us
    pallas_call x1, Pallas kernels, _reorder(): pl.pallas_call(_reorder_kernel, grid_spec=pltpu.PrefetchScalarGridSpec(nu...  6.51 us
    dot_general x4, matrix products, _dot_rows(): lax.dot_general(block, rows, (((1,), (1,)), ((), ())), preferred_element_...  5.15 us
  transfers between devices with their start and end apart: 30, of which 10 were waited for; matrix products, arithmetic and copies ran while one was open for 5% of the time, Pallas kernels for 14%

commit v1 on v0

--- a/solution.py
+++ b/solution.py
@@ -62,7 +62,7 @@
 def _near_scores(total, after, before, rows):
     count, wide = after.shape
     tile = rows.shape[0] // SIDE
-    panel = pl.BlockSpec((count, wide), lambda i: (0, 0))
+    panel = pl.BlockSpec(memory_space=pltpu.VMEM)
     tiles = pl.BlockSpec((count, tile), lambda i: (0, i))
     return pl.pallas_call(
         _near_scores_kernel,
@@ -85,13 +85,15 @@
     )(total, after, before, rows, rows)
 
 
-def _gather_scores(axis, panel, rows):
+def _gather_weights(axis, panel, rows):
     after, far, before = _ring(panel, axis)
     wide = panel.shape[1]
     total = _dot_rows(rows[:, :wide], panel)
     total = _near_scores(total, after, before, rows)
     squares = _squares(panel) + _squares(after) + _squares(before) + _squares(far)
-    return total + _dot_rows(rows[:, 2 * wide : 3 * wide], far), squares
+    scores = total + _dot_rows(rows[:, 2 * wide : 3 * wide], far)
+    weights = jnp.exp(scores * lax.rsqrt(squares + 1e-06)[:, None] * 20.0)
+    return weights, jnp.sum(weights, 1)
 
 
 def _pack(value):
@@ -106,12 +108,13 @@
 FULL = lax.Precision.HIGHEST
 
 
-def _chunks(count, body):
-    def step(i, carry):
-        body(pl.ds(pl.multiple_of(i * CHUNK, CHUNK), CHUNK))
-        return carry
-
-    lax.fori_loop(0, count // CHUNK, step, 0, unroll=True)
+def _chunks(refs):
+    base = 0
+    for ref in refs:
+        for start in range(0, ref.shape[0], CHUNK):
+            whole = slice(base + start, base + start + CHUNK)
+            yield ref, slice(start, start + CHUNK), whole
+        base += ref.shape[0]
 
 
 def _column_chunk(row_ref, cut, count):
@@ -130,49 +133,36 @@
     )
 
 
-def _row_sums_kernel(target, weights_ref, column_ref, out_ref, scale_ref, total_ref):
+def _row_sums_kernel(target, a_ref, b_ref, column_ref, out_ref, scale_ref):
     scale_ref[...] = target / jnp.sum(column_ref[...], 0)
-    count, rows = weights_ref.shape
-    total_ref[...] = jnp.zeros_like(total_ref)
-
-    def body(cut):
-        chunk = weights_ref[cut, :] * _column_chunk(scale_ref, cut, rows)
-        total_ref[...] += jnp.sum(chunk.reshape(CHUNK // 8, 8, rows), 0)
-
-    _chunks(count, body)
-    total = jnp.sum(total_ref[...], 0, keepdims=True)
+    rows = a_ref.shape[1]
+    total = jnp.zeros((8, rows), jnp.float32)
+    for ref, cut, whole in _chunks((a_ref, b_ref)):
+        chunk = ref[cut, :] * _column_chunk(scale_ref, whole, rows)
+        total = total + jnp.sum(chunk.reshape(CHUNK // 8, 8, rows), 0)
+    total = jnp.sum(total, 0, keepdims=True)
     out_ref[...] = jnp.broadcast_to(total[None], out_ref.shape)
 
 
-def _column_sums_kernel(weights_ref, row_ref, out_ref, scale_ref):
-    scale_ref[...] = 1.0 / jnp.sum(row_ref[...], 0)
-
-    def body(cut):
-        folded = _fold(weights_ref[cut, :] * scale_ref[...])
-        out_ref[:, 0, cut] = _lane_sums(folded, out_ref.shape[0])
-
-    _chunks(weights_ref.shape[0], body)
-
-
-def _shares_kernel(
-    target, weights_ref, column_ref, row_ref, shares_ref, mass_ref, column_scale_ref, row_scale_ref
-):
-    column_scale_ref[...] = target / jnp.sum(column_ref[...], 0)
-    row_scale_ref[...] = 1.0 / jnp.sum(row_ref[...], 0)
-    count, rows = weights_ref.shape
-
-    def body(cut):
-        scale = _column_chunk(column_scale_ref, cut, rows) * row_scale_ref[...]
-        shares = (weights_ref[cut, :] * scale).astype(jnp.bfloat16)
-        shares_ref[cut, :] = shares
-        column_scale_ref[:, cut] = _lane_sums(_fold(shares.astype(jnp.float32)), 8)[:1]
-
-    _chunks(count, body)
+def _column_sums_kernel(a_ref, b_ref, row_ref, out_ref):
+    scale = 1.0 / jnp.sum(row_ref[...], 0)
+    for ref, cut, whole in _chunks((a_ref, b_ref)):
+        out_ref[:, 0, whole] = _lane_sums(_fold(ref[cut, :] * scale), out_ref.shape[0])
+
+
+def _shares_kernel(target, a_ref, b_ref, column_ref, row_ref, shares_ref, mass_ref, scale_ref):
+    scale_ref[...] = target / jnp.sum(column_ref[...], 0)
+    row_scale = 1.0 / jnp.sum(row_ref[...], 0)
     mass_ref[...] = jnp.zeros_like(mass_ref)
     halves, _, width = mass_ref.shape
-    for start in range(0, count, width):
-        half, place = divmod(start, count // halves)
-        mass_ref[half, place // width] = column_scale_ref[0, start : start + width]
+    for ref, cut, whole in _chunks((a_ref, b_ref)):
+        scale = _column_chunk(scale_ref, whole, ref.shape[1]) * row_scale
+        shares = (ref[cut, :] * scale).astype(jnp.bfloat16)
+        shares_ref[whole, :] = shares
+        mass = _lane_sums(_fold(shares.astype(jnp.float32)), 8)
+        half, place = divmod(whole.start, shares_ref.shape[0] // halves)
+        row, lane = divmod(place, width)
+        mass_ref[half, row, lane : lane + CHUNK] = mass[0]
 
 
 def _whole(kernel, out_shape, scratch, *operands):
@@ -195,35 +185,35 @@
     return lax.all_to_all(copies, axis, 0, 0)
 
 
-def _part_kernel(slots_ref, shares_ref, mass_ref, rows_ref, part_ref):
-    count = shares_ref.shape[0]
-    part_ref[0, :count] = jnp.dot(shares_ref[...], rows_ref[0], preferred_element_type=jnp.float32)
-    part_ref[0, count:] = mass_ref[0]
+def _part_kernel(halves, slots_ref, shares_ref, mass_ref, rows_ref, part_ref):
+    count = shares_ref.shape[0] // 2
+    each = part_ref.shape[0] // len(halves)
+    for h, half in enumerate(halves):
+        cut = slice(half * count, (half + 1) * count)
+
+        def body(i, carry):
+            i = h * each + i
+            part_ref[i, :count] = jnp.dot(
+                shares_ref[cut, :], rows_ref[slots_ref[i]], preferred_element_type=jnp.float32
+            )
+            part_ref[i, count:] = mass_ref[half]
+            return carry
+
+        lax.fori_loop(0, each, body, 0)
 
 
 def _part(shares, mass, halves, blocks, slots, flops=1000):
-    count, rows = shares.shape[0] // 2, shares.shape[1]
-    width = blocks.shape[2]
-    extra = mass.shape[1]
-    first, each = halves[0], slots[0].shape[0]
+    count = shares.shape[0] // 2 + mass.shape[1]
+    inside = pl.BlockSpec(memory_space=pltpu.VMEM)
+    slots = jnp.concatenate(slots)
     return pl.pallas_call(
-        _part_kernel,
-        grid_spec=pltpu.PrefetchScalarGridSpec(
-            num_scalar_prefetch=1,
-            grid=(len(halves), each),
-            in_specs=[
-                pl.BlockSpec((count, rows), lambda h, i, slots: (first + h, 0)),
-                pl.BlockSpec((1, extra, width), lambda h, i, slots: (first + h, 0, 0)),
-                pl.BlockSpec((1, rows, width), lambda h, i, slots: (slots[h * each + i], 0, 0)),
-            ],
-            out_specs=pl.BlockSpec(
-                (1, count + extra, width), lambda h, i, slots: (h * each + i, 0, 0)
-            ),
-        ),
-        out_shape=jax.ShapeDtypeStruct((len(halves) * each, count + extra, width), jnp.float32),
+        functools.partial(_part_kernel, halves),
+        in_specs=[pl.BlockSpec(memory_space=pltpu.SMEM), inside, inside, inside],
+        out_specs=inside,
+        out_shape=jax.ShapeDtypeStruct((slots.size, count, blocks.shape[2]), jnp.float32),
         cost_estimate=pl.CostEstimate(flops=flops, bytes_accessed=flops // 512, transcendentals=0),
-        compiler_params=pltpu.CompilerParams(vmem_limit_bytes=8 * 1024 * 1024),
-    )(jnp.concatenate(slots), shares, mass, blocks)
+        compiler_params=pltpu.CompilerParams(vmem_limit_bytes=24 * 1024 * 1024),
+    )(slots, shares, mass, blocks)
 
 
 def _ring_far(part, axis):
@@ -250,15 +240,32 @@
     shares, packed = lax.optimization_barrier((shares, packed))
     near = [_part(shares, mass, [half], blocks, [slots[half][1]]) for half in range(2)]
     own = _part(shares, mass, [0, 1], blocks, [slot[2] for slot in slots])
-    out = []
-    for half, (first, second) in enumerate(axes):
-        ends = _ring_near(near[half][:SIDE], near[half][SIDE:], far[half], first)
-        line = [
-            own[SIDE * half + i] + _unpack(ends[0][i]) + _unpack(ends[1][i]) for i in range(SIDE)
-        ]
-        came = [_send(_pack(line[i]), second, i) for i in (1, 3, 2)]
-        out.append(line[0] + _unpack(came[0]) + _unpack(came[1]) + _unpack(came[2]))
-    return out
+    ends = [
+        _ring_near(near[half][:SIDE], near[half][SIDE:], far[half], first)
+        for half, (first, _) in enumerate(axes)
+    ]
+    lines, came = [], []
+    for half, (_, second) in enumerate(axes):
+        line = _line(own, half, ends[half])
+        packed = [_pack(line[i]) for i in (1, 3, 2)]
+        if half == 0:
+            ends[1], packed = lax.optimization_barrier((ends[1], packed))
+        lines.append(line[0])
+        came.append([_send(block, second, i) for i, block in zip((1, 3, 2), packed)])
+    first = _means(lines[0], came[0])
+    came[1], first = lax.optimization_barrier((came[1], first))
+    return first, _means(lines[1], came[1])
+
+
+def _line(own, half, ends):
+    return [own[SIDE * half + i] + _unpack(ends[0][i]) + _unpack(ends[1][i]) for i in range(SIDE)]
+
+
+def _means(own, came):
+    total = own + _unpack(came[0]) + _unpack(came[1]) + _unpack(came[2])
+    count = total.shape[0] - MASS_ROWS
+    mass = total[count:].reshape(-1)[:count]
+    return (total[:count] / mass[:, None]).astype(jnp.bfloat16)
 
 
 def _place(place_ref, value, by_x_ref, by_z_ref):
@@ -325,28 +332,27 @@
     place = jnp.stack([x, z]).astype(jnp.int32)
     panel_a = _line_panel(_z, centroids[:half])
     panel_b = _line_panel(_x, centroids[half:])
-    place, slots, panel_a, panel_b = lax.optimization_barrier((place, slots, panel_a, panel_b))
+    place, slots, _ = lax.optimization_barrier((place, slots, (panel_a, panel_b)))
     normed_x, normed_z, blocks = _reorder(embeddings, place)
-    score_a, square_a = _gather_scores(_x, panel_a, normed_x)
-    score_b, square_b = _gather_scores(_z, panel_b, normed_z)
-    scores = jnp.concatenate([score_a, score_b], 0)
-    scale = lax.rsqrt(jnp.concatenate([square_a, square_b]) + 1e-06)
-    weights = jnp.exp(scores * scale[:, None] * 20.0)
+    weights_a, sums_a = _gather_weights(_x, panel_a, normed_x)
+    weights_b, sums_b = _gather_weights(_z, panel_b, normed_z)
     target = row_count * lax.axis_size("dp") / (local_k * lax.axis_size("cent"))
-    column = jnp.broadcast_to(jnp.sum(weights, 1)[None, None], _copies("dp", local_k).shape)
+    column = jnp.concatenate([sums_a, sums_b])
+    column = jnp.broadcast_to(column[None, None], _copies("dp", local_k).shape)
     for sweep in range(ROUNDS):
         column = _exchange(column, "dp")
         row = _whole(
             functools.partial(_row_sums_kernel, target),
             _copies("cent", row_count),
-            [(1, local_k), (8, row_count)],
-            weights,
+            [(1, local_k)],
+            weights_a,
+            weights_b,
             column,
         )
         row = _exchange(row, "cent")
         if sweep + 1 < ROUNDS:
             column = _whole(
-                _column_sums_kernel, _copies("dp", local_k), [(1, row_count)], weights, row
+                _column_sums_kernel, _copies("dp", local_k), [], weights_a, weights_b, row
             )
     width = centroids.shape[1]
     shares, mass = _whole(
@@ -355,18 +361,15 @@
             jax.ShapeDtypeStruct((local_k, row_count), jnp.bfloat16),
             jax.ShapeDtypeStruct((2, MASS_ROWS, width), jnp.float32),
         ),
-        [(1, local_k), (1, row_count)],
-        weights,
+        [(1, local_k)],
+        weights_a,
+        weights_b,
         column,
         row,
     )
-    sums = _scatter_sums(shares, mass, [(_x, _z), (_z, _x)], blocks, slots)
-    means = []
-    for total in sums:
-        mass = total[half:].reshape(-1)[:half]
-        means.append((total[:half] / mass[:, None]).astype(jnp.bfloat16))
-    first = lax.optimization_barrier(jnp.pad(means[0], ((0, half), (0, 0))))
-    return (shares.T, lax.dynamic_update_slice(first, means[1], (half, 0)))
+    first, second = _scatter_sums(shares, mass, [(_x, _z), (_z, _x)], blocks, slots)
+    first = jnp.pad(first, ((0, half), (0, 0)))
+    return (shares.T, lax.dynamic_update_slice(first, second, (half, 0)))
 
 
 def solution(mesh):

time: 204 us -> 202 us (level)
  waiting for transfers between devices: 36.6 us -> 30 us
  other arithmetic: 11.7 us -> 17.2 us
    ppermute x30, waiting for transfers between devices: 36.6 us -> 30 us  [_send(): return lax.ppermute(value, 'dp', axis(step))]
    convert_element_type x5 -> x6, other arithmetic: 3.81 us -> 8.84 us  [_pack(): return (value * PACK).astype(jnp.float16)]
    unnamed x19 -> x11, local copies, waits for them, and re-layouts: 6.8 us -> 7.97 us
  transfers between devices with their start and end apart: 30 -> 30, of which waited for: 10 -> 14; matrix products, arithmetic and copies ran while one was open for 5% -> 10% of each run, Pallas kernels for 14% -> 14%
where the time goes in v1:
time: 202 us
  blocking collectives  57.5 us (28%)
  starting transfers between devices  46.3 us (23%)
  Pallas kernels  35.1 us (17%)
  waiting for transfers between devices  30 us (15%)
  other arithmetic  17.2 us (9%)
  local copies, waits for them, and re-layouts  9.34 us (5%)
  matrix products  5.18 us (3%)
    all_to_all x6, blocking collectives, _exchange(): return lax.all_to_all(copies, axis, 0, 0)  57.5 us
    ppermute x30, starting transfers between devices, _send(): return lax.ppermute(value, 'dp', axis(step))  46.3 us
    ppermute x30, waiting for transfers between devices, _send(): return lax.ppermute(value, 'dp', axis(step))  30 us
    pallas_call x5, Pallas kernels, _part(): pl.pallas_call(functools.partial(_part_kernel, halves), in_specs=[pl.Bloc...  16.8 us
    convert_element_type x6, other arithmetic, _pack(): return (value * PACK).astype(jnp.float16)  8.84 us
    unnamed x11, local copies, waits for them, and re-layouts  7.97 us
    pallas_call x2, Pallas kernels, _near_scores(): pl.pallas_call(_near_scores_kernel, grid=(SIDE,), in_specs=[tiles, panel,...  7.19 us
    pallas_call x1, Pallas kernels, _reorder(): pl.pallas_call(_reorder_kernel, grid_spec=pltpu.PrefetchScalarGridSpec(nu...  6.45 us
  transfers between devices with their start and end apart: 30, of which 14 were waited for; matrix products, arithmetic and copies ran while one was open for 10% of the time, Pallas kernels for 14%

profile of v1, /device:TPU:0, one launch (start us, length us, event | category | flops | bytes accessed | tf_op | source)
XLA Modules:
  0.0 201.8 jit_solution(5735144732422455628)
XLA Ops:
  9.3 2.4 %collective-permute-done = bf16[512,256]{1,0:T(8,128)(2,1)S(1)} collective-permute-done((bf16[512,256]{1,0:T(8,128)(2,1)S(1)}, bf16[512,256]{1,0:T(8,128)(2,1)S(1)}, u32[]{:S(2)}, u32[]{:S(2)}) %collective-permute-start) | collective-permute-done | bytes 262176 | tf_op jit(solution)/shard_map/ppermute | solution.py:29
  11.7 3.6 %collective-permute-start.3 = (bf16[256,256]{1,0:T(8,128)(2,1)S(1)}, bf16[256,256]{1,0:T(8,128)(2,1)S(1)}, u32[]{:S(2)}, u32[]{:S(2)}) collective-permute-start(bf16[256,256]{1,0:T(8,128)(2,1)S(1)} %slice.239), channel_id=1, source_target_pairs={{0,24},{8,0},{16,8},{24,16},{32,56},{40,32},{48,40},{56,48},{64,88... | collective-permute-start | bytes 393224 | tf_op jit(solution)/shard_map/ppermute | solution.py:29
  15.5 2.8 %collective-permute-start.7 = (bf16[256,256]{1,0:T(8,128)(2,1)S(1)}, bf16[256,256]{1,0:T(8,128)(2,1)S(1)}, u32[]{:S(2)}, u32[]{:S(2)}) collective-permute-start(bf16[256,256]{1,0:T(8,128)(2,1)S(1)} %slice.241), channel_id=1, source_target_pairs={{0,96},{8,104},{16,112},{24,120},{32,0},{40,8},{48,16},{56,24},{64... | collective-permute-start | bytes 393224 | tf_op jit(solution)/shard_map/ppermute | solution.py:29
  18.4 3.2 %collective-permute-done.2 = bf16[256,256]{1,0:T(8,128)(2,1)S(1)} collective-permute-done((bf16[256,256]{1,0:T(8,128)(2,1)S(1)}, bf16[256,256]{1,0:T(8,128)(2,1)S(1)}, u32[]{:S(2)}, u32[]{:S(2)}) %collective-permute-start.2) | collective-permute-done | bytes 131104 | tf_op jit(solution)/shard_map/ppermute | solution.py:29
  26.5 3.2 %collective-permute-start.12 = (bf16[512,1024]{1,0:T(8,128)(2,1)S(1)}, bf16[512,1024]{1,0:T(8,128)(2,1)S(1)}, u32[]{:S(2)}, u32[]{:S(2)}) collective-permute-start(bf16[512,1024]{1,0:T(8,128)(2,1)S(1)} %get-tuple-element.53), channel_id=1, source_target_pairs={{0,24},{8,0},{16,8},{24,16},{32,56},{40,32},{48,40},{56,48},{64,88... | collective-permute-start | bytes 3145736 | tf_op jit(solution)/shard_map/ppermute | solution.py:29
  29.9 3.4 %copy-done.1 = bf16[1024,4096]{1,0:T(8,128)(2,1)S(1)} copy-done((bf16[1024,4096]{1,0:T(8,128)(2,1)S(1)}, bf16[1024,4096]{1,0:T(8,128)(2,1)}, u32[]{:S(2)}) %copy-start.1) | copy-done | bytes 8388632
  33.3 6.5 %shard_map.41 = (bf16[1024,4096]{1,0:T(8,128)(2,1)S(1)}, bf16[1024,4096]{1,0:T(8,128)(2,1)S(1)}, bf16[16,1024,256]{2,1,0:T(8,128)(2,1)S(1)}) custom-call(s32[2]{0:T(128)S(1)} %pad_add_fusion.place_ref, bf16[1024,4096]{1,0:T(8,128)(2,1)S(1)} %copy-done.1), custom_call_target="tpu_custom_call" | custom-call | flops 12582912 | bytes 33554432 | tf_op jit(solution)/shard_map/pallas_call | solution.py:299
  42.3 4.7 %collective-permute-done.9.before_ref = bf16[512,1024]{1,0:T(8,128)(2,1)S(1)} collective-permute-done((bf16[512,1024]{1,0:T(8,128)(2,1)S(1)}, bf16[512,1024]{1,0:T(8,128)(2,1)S(1)}, u32[]{:S(2)}, u32[]{:S(2)}) %collective-permute-start.9) | collective-permute-done | bytes 1048608 | tf_op jit(solution)/shard_map/ppermute | solution.py:29
  47.2 3.3 %collective-permute-start.11 = (bf16[256,1024]{1,0:T(8,128)(2,1)S(1)}, bf16[256,1024]{1,0:T(8,128)(2,1)S(1)}, u32[]{:S(2)}, u32[]{:S(2)}) collective-permute-start(bf16[256,1024]{1,0:T(8,128)(2,1)S(1)} %slice.243), channel_id=1, source_target_pairs={{0,96},{8,104},{16,112},{24,120},{32,0},{40,8},{48,16},{56,24},{64... | collective-permute-start | bytes 1572872 | tf_op jit(solution)/shard_map/ppermute | solution.py:29
  50.6 3.5 %collective-permute-start.15 = (bf16[256,1024]{1,0:T(8,128)(2,1)S(1)}, bf16[256,1024]{1,0:T(8,128)(2,1)S(1)}, u32[]{:S(2)}, u32[]{:S(2)}) collective-permute-start(bf16[256,1024]{1,0:T(8,128)(2,1)S(1)} %slice.245), channel_id=1, source_target_pairs={{0,24},{8,0},{16,8},{24,16},{32,56},{40,32},{48,40},{56,48},{64,88... | collective-permute-start | bytes 1572872 | tf_op jit(solution)/shard_map/ppermute | solution.py:29
  54.7 3.6 %shard_map.42 = f32[512,1024]{1,0:T(8,128)S(1)} custom-call(f32[512,1024]{1,0:T(8,128)S(1)} %fusion.14.total_ref, bf16[512,1024]{1,0:T(8,128)(2,1)S(1)} %collective-permute-done.8.after_ref, bf16[512,1024]{1,0:T(8,128)(2,1)S(1)} %collective-permute-done.9.before_ref, bf16[1024,4096]{1,0:T(8,128)(2,1)S(1)} %get-tuple-element.25.rows_1_ref.rows_3_ref, ...), custom_call_target="tpu_custom_call" | custom-call | flops 2147483648 | bytes 10485760 | tf_op jit(solution)/shard_map/pallas_call | solution.py:67
  58.8 3.6 %shard_map.43 = f32[512,1024]{1,0:T(8,128)S(1)} custom-call(f32[512,1024]{1,0:T(8,128)S(1)} %fusion.10.total_ref, bf16[512,1024]{1,0:T(8,128)(2,1)S(1)} %collective-permute-done.12.after_ref, bf16[512,1024]{1,0:T(8,128)(2,1)S(1)} %collective-permute-done.13.before_ref, bf16[1024,4096]{1,0:T(8,128)(2,1)S(1)} %get-tuple-element.26.rows_1_ref.rows_3_ref, ...), custom_call_target="tpu_custom_call" | custom-call | flops 2147483648 | bytes 10485760 | tf_op jit(solution)/shard_map/pallas_call | solution.py:67
  67.6 10.4 %all_to_all.30.column_ref = f32[16,1,1024]{2,1,0:T(1,128)S(1)} all-to-all(f32[16,1,1024]{2,1,0:T(1,128)S(1)} %broadcast_in_dim.2), channel_id=1, replica_groups=mesh['dp'=16,'cent'=8] {'dp'}, dimensions={0} | all-to-all | bytes 131072 | tf_op jit(solution)/shard_map/all_to_all | solution.py:185
  78.4 9.7 %all_to_all.31.row_ref = f32[8,1,1024]{2,1,0:T(1,128)S(1)} all-to-all(f32[8,1,1024]{2,1,0:T(1,128)S(1)} %shard_map.44), channel_id=1, replica_groups=mesh['dp'=16,'cent'=8] {'cent'}, dimensions={0} | all-to-all | bytes 65536 | tf_op jit(solution)/shard_map/all_to_all | solution.py:185
  89.1 10.9 %all_to_all.32.column_ref = f32[16,1,1024]{2,1,0:T(1,128)S(1)} all-to-all(f32[16,1,1024]{2,1,0:T(1,128)S(1)} %shard_map.45), channel_id=1, replica_groups=mesh['dp'=16,'cent'=8] {'dp'}, dimensions={0} | all-to-all | bytes 131072 | tf_op jit(solution)/shard_map/all_to_all | solution.py:185
  100.4 7.8 %all_to_all.33.row_ref = f32[8,1,1024]{2,1,0:T(1,128)S(1)} all-to-all(f32[8,1,1024]{2,1,0:T(1,128)S(1)} %shard_map.46), channel_id=1, replica_groups=mesh['dp'=16,'cent'=8] {'cent'}, dimensions={0} | all-to-all | bytes 65536 | tf_op jit(solution)/shard_map/all_to_all | solution.py:185
  109.3 10.9 %all_to_all.34.column_ref = f32[16,1,1024]{2,1,0:T(1,128)S(1)} all-to-all(f32[16,1,1024]{2,1,0:T(1,128)S(1)} %shard_map.47), channel_id=1, replica_groups=mesh['dp'=16,'cent'=8] {'dp'}, dimensions={0} | all-to-all | bytes 131072 | tf_op jit(solution)/shard_map/all_to_all | solution.py:185
  120.6 7.8 %all_to_all.35.row_ref = f32[8,1,1024]{2,1,0:T(1,128)S(1)} all-to-all(f32[8,1,1024]{2,1,0:T(1,128)S(1)} %shard_map.48), channel_id=1, replica_groups=mesh['dp'=16,'cent'=8] {'cent'}, dimensions={0} | all-to-all | bytes 65536 | tf_op jit(solution)/shard_map/all_to_all | solution.py:185
  129.8 2.3 %shard_map.50 = f32[4,528,256]{2,1,0:T(8,128)S(1)} custom-call(s32[4]{0:T(128)S(1)} %get-tuple-element.30.slots_ref, bf16[1024,1024]{1,0:T(8,128)(2,1)S(1)} %get-tuple-element.34.shares_ref, f32[2,16,256]{2,1,0:T(8,128)S(1)} %get-tuple-element.31.mass_ref, bf16[16,1024,256]{2,1,0:T(8,128)(2,1)S(1)} %get-tuple-element.32.rows_ref), custom_call_target="tpu_custom_call" | custom-call | flops 2147483648 | bytes 4194304 | tf_op jit(solution)/shard_map/pallas_call | solution.py:209
  133.0 2.7 %collective-permute-start.22 = (f16[2,528,256]{2,1,0:T(8,128)(2,1)S(1)}, f16[2,528,256]{2,1,0:T(8,128)(2,1)S(1)}, u32[]{:S(2)}, u32[]{:S(2)}) collective-permute-start(f16[2,528,256]{2,1,0:T(8,128)(2,1)S(1)} %get-tuple-element.68), channel_id=1, source_target_pairs={{0,96},{8,104},{16,112},{24,120},{32,0},{40,8},{48,16},{56,24},{64... | collective-permute-start | bytes 1622024 | tf_op jit(solution)/shard_map/ppermute | solution.py:29
  135.7 2.3 %shard_map.51 = f32[4,528,256]{2,1,0:T(8,128)S(1)} custom-call(s32[4]{0:T(128)S(1)} %get-tuple-element.33.slots_ref, bf16[1024,1024]{1,0:T(8,128)(2,1)S(1)} %get-tuple-element.34.shares_ref, f32[2,16,256]{2,1,0:T(8,128)S(1)} %get-tuple-element.31.mass_ref, bf16[16,1024,256]{2,1,0:T(8,128)(2,1)S(1)} %get-tuple-element.32.rows_ref), custom_call_target="tpu_custom_call" | custom-call | flops 2147483648 | bytes 4194304 | tf_op jit(solution)/shard_map/pallas_call | solution.py:209
  140.4 4.1 %shard_map.53 = f32[8,528,256]{2,1,0:T(8,128)S(1)} custom-call(s32[8]{0:T(128)S(1)} %pad_add_fusion.2.slots_ref, bf16[1024,1024]{1,0:T(8,128)(2,1)S(1)} %get-tuple-element.34.shares_ref, f32[2,16,256]{2,1,0:T(8,128)S(1)} %get-tuple-element.31.mass_ref, bf16[16,1024,256]{2,1,0:T(8,128)(2,1)S(1)} %get-tuple-element.32.rows_ref), custom_call_target="tpu_custom_call" | custom-call | flops 1000 | bytes 1 | tf_op jit(solution)/shard_map/pallas_call | solution.py:209
  144.4 4.1 %shard_map.54 = f32[8,528,256]{2,1,0:T(8,128)S(1)} custom-call(s32[8]{0:T(128)S(1)} %pad_add_fusion.1.slots_ref, bf16[1024,1024]{1,0:T(8,128)(2,1)S(1)} %get-tuple-element.34.shares_ref, f32[2,16,256]{2,1,0:T(8,128)S(1)} %get-tuple-element.31.mass_ref, bf16[16,1024,256]{2,1,0:T(8,128)(2,1)S(1)} %get-tuple-element.32.rows_ref), custom_call_target="tpu_custom_call" | custom-call | flops 1000 | bytes 1 | tf_op jit(solution)/shard_map/pallas_call | solution.py:209
  156.0 3.2 %collective-permute-start.19 = (f16[4,528,256]{2,1,0:T(8,128)(2,1)}, f16[4,528,256]{2,1,0:T(8,128)(2,1)}, u32[]{:S(2)}, u32[]{:S(2)}) collective-permute-start(f16[4,528,256]{2,1,0:T(8,128)(2,1)} %get-tuple-element.64), channel_id=1, source_target_pairs={{0,24},{8,0},{16,8},{24,16},{32,56},{40,32},{48,40},{56,48},{64,88... | collective-permute-start | bytes 3244040 | tf_op jit(solution)/shard_map/ppermute | solution.py:29
  159.3 4.1 %shard_map.52 = f32[8,528,256]{2,1,0:T(8,128)S(1)} custom-call(s32[8]{0:T(128)S(1)} %pad_add_fusion.3.slots_ref, bf16[1024,1024]{1,0:T(8,128)(2,1)S(1)} %get-tuple-element.34.shares_ref, f32[2,16,256]{2,1,0:T(8,128)S(1)} %get-tuple-element.31.mass_ref, bf16[16,1024,256]{2,1,0:T(8,128)(2,1)S(1)} %get-tuple-element.32.rows_ref), custom_call_target="tpu_custom_call" | custom-call | flops 1000 | bytes 1 | tf_op jit(solution)/shard_map/pallas_call | solution.py:209
  165.4 2.5 %copy.4 = bf16[1024,1024]{1,0:T(8,128)(2,1)} copy(bf16[1024,1024]{0,1:T(8,128)(2,1)S(1)} %bitcast.57) | data formatting | bytes 4194304
  167.9 7.3 %collective-permute-done.23 = f16[4,528,256]{2,1,0:T(8,128)(2,1)} collective-permute-done((f16[4,528,256]{2,1,0:T(8,128)(2,1)}, f16[4,528,256]{2,1,0:T(8,128)(2,1)}, u32[]{:S(2)}, u32[]{:S(2)}) %collective-permute-start.23) | collective-permute-done | bytes 1081376 | tf_op jit(solution)/shard_map/ppermute | solution.py:29
  175.2 2.6 %collective-permute-done.21 = f16[4,528,256]{2,1,0:T(8,128)(2,1)} collective-permute-done((f16[4,528,256]{2,1,0:T(8,128)(2,1)S(1)}, f16[4,528,256]{2,1,0:T(8,128)(2,1)}, u32[]{:S(2)}, u32[]{:S(2)}) %collective-permute-start.21) | collective-permute-done | bytes 1081376 | tf_op jit(solution)/shard_map/ppermute | solution.py:29
  177.8 2.3 %fusion.53 = (f16[528,256]{1,0:T(8,128)(2,1)S(1)}, f16[528,256]{1,0:T(8,128)(2,1)S(1)}, f16[528,256]{1,0:T(8,128)(2,1)S(1)}) fusion(f32[8,528,256]{2,1,0:T(8,128)} %copy-done, f16[4,528,256]{2,1,0:T(8,128)(2,1)} %collective-permute-done.23, f16[4,528,256]{2,1,0:T(8,128)(2,1)} %collective-permute-done.21), kind=kLoop, calls=%fused_computation.88 | loop fusion | flops 3244032 | bytes 4055040 | tf_op jit(solution)/shard_map/convert_element_type | solution.py:100
  185.2 2.3 %fusion.55 = (f16[528,256]{1,0:T(8,128)(2,1)S(1)}, f16[528,256]{1,0:T(8,128)(2,1)S(1)}, f16[528,256]{1,0:T(8,128)(2,1)S(1)}) fusion(f32[8,528,256]{2,1,0:T(8,128)} %copy-done, f16[4,528,256]{2,1,0:T(8,128)(2,1)} %collective-permute-done.19, f16[4,528,256]{2,1,0:T(8,128)(2,1)} %collective-permute-done.17), kind=kLoop, calls=%fused_computation.90 | loop fusion | flops 3244032 | bytes 4055040 | tf_op jit(solution)/shard_map/convert_element_type | solution.py:100
  187.5 3.2 %collective-permute-start.25 = (f16[528,256]{1,0:T(8,128)(2,1)S(1)}, f16[528,256]{1,0:T(8,128)(2,1)S(1)}, u32[]{:S(2)}, u32[]{:S(2)}) collective-permute-start(f16[528,256]{1,0:T(8,128)(2,1)S(1)} %get-tuple-element.57), channel_id=1, source_target_pairs={{0,96},{8,104},{16,112},{24,120},{32,0},{40,8},{48,16},{56,24},{64... | collective-permute-start | bytes 811016 | tf_op jit(solution)/shard_map/ppermute | solution.py:29
  192.0 2.2 %collective-permute-done.28 = f16[528,256]{1,0:T(8,128)(2,1)S(1)} collective-permute-done((f16[528,256]{1,0:T(8,128)(2,1)S(1)}, f16[528,256]{1,0:T(8,128)(2,1)S(1)}, u32[]{:S(2)}, u32[]{:S(2)}) %collective-permute-start.28) | collective-permute-done | bytes 270368 | tf_op jit(solution)/shard_map/ppermute | solution.py:29
  (111 shorter events, 54.3 us)
Async XLA Ops:
  1.7 13.6 %collective-permute-start.1 = (bf16[512,256]{1,0:T(8,128)(2,1)S(1)}, bf16[512,256]{1,0:T(8,128)(2,1)S(1)}, u32[]{:S(2)}, u32[]{:S(2)}) collective-permute-start(bf16[512,256]{1,0:T(8,128)(2,1)S(1)} %get-tuple-element.71), channel_id=1, source_target_pairs={{0,8},{8,16},{16,24},{24,0},{32,40},{40,48},{48,56},{56,32},{64,72... | collective-permute-start | bytes 786440 | tf_op jit(solution)/shard_map/ppermute | solution.py:29
  3.8 7.9 %collective-permute-start = (bf16[512,256]{1,0:T(8,128)(2,1)S(1)}, bf16[512,256]{1,0:T(8,128)(2,1)S(1)}, u32[]{:S(2)}, u32[]{:S(2)}) collective-permute-start(bf16[512,256]{1,0:T(8,128)(2,1)S(1)} %get-tuple-element.71), channel_id=1, source_target_pairs={{0,24},{8,0},{16,8},{24,16},{32,56},{40,32},{48,40},{56,48},{64,88... | collective-permute-start | bytes 786440 | tf_op jit(solution)/shard_map/ppermute | solution.py:29
  6.0 12.3 %collective-permute-start.5 = (bf16[512,256]{1,0:T(8,128)(2,1)S(1)}, bf16[512,256]{1,0:T(8,128)(2,1)S(1)}, u32[]{:S(2)}, u32[]{:S(2)}) collective-permute-start(bf16[512,256]{1,0:T(8,128)(2,1)S(1)} %get-tuple-element.70), channel_id=1, source_target_pairs={{0,32},{8,40},{16,48},{24,56},{32,64},{40,72},{48,80},{56,88},{64,... | collective-permute-start | bytes 786440 | tf_op jit(solution)/shard_map/ppermute | solution.py:29
  7.5 8.0 %collective-permute-start.4 = (bf16[512,256]{1,0:T(8,128)(2,1)S(1)}, bf16[512,256]{1,0:T(8,128)(2,1)S(1)}, u32[]{:S(2)}, u32[]{:S(2)}) collective-permute-start(bf16[512,256]{1,0:T(8,128)(2,1)S(1)} %get-tuple-element.70), channel_id=1, source_target_pairs={{0,96},{8,104},{16,112},{24,120},{32,0},{40,8},{48,16},{56,24},{64... | collective-permute-start | bytes 786440 | tf_op jit(solution)/shard_map/ppermute | solution.py:29
  11.7 6.7 %collective-permute-start.3 = (bf16[256,256]{1,0:T(8,128)(2,1)S(1)}, bf16[256,256]{1,0:T(8,128)(2,1)S(1)}, u32[]{:S(2)}, u32[]{:S(2)}) collective-permute-start(bf16[256,256]{1,0:T(8,128)(2,1)S(1)} %slice.239), channel_id=1, source_target_pairs={{0,24},{8,0},{16,8},{24,16},{32,56},{40,32},{48,40},{56,48},{64,88... | collective-permute-start | bytes 393224 | tf_op jit(solution)/shard_map/ppermute | solution.py:29
  15.3 6.2 %collective-permute-start.2 = (bf16[256,256]{1,0:T(8,128)(2,1)S(1)}, bf16[256,256]{1,0:T(8,128)(2,1)S(1)}, u32[]{:S(2)}, u32[]{:S(2)}) collective-permute-start(bf16[256,256]{1,0:T(8,128)(2,1)S(1)} %slice.238), channel_id=1, source_target_pairs={{0,8},{8,16},{16,24},{24,0},{32,40},{40,48},{48,56},{56,32},{64,72... | collective-permute-start | bytes 393224 | tf_op jit(solution)/shard_map/ppermute | solution.py:29
  15.5 9.7 %collective-permute-start.7 = (bf16[256,256]{1,0:T(8,128)(2,1)S(1)}, bf16[256,256]{1,0:T(8,128)(2,1)S(1)}, u32[]{:S(2)}, u32[]{:S(2)}) collective-permute-start(bf16[256,256]{1,0:T(8,128)(2,1)S(1)} %slice.241), channel_id=1, source_target_pairs={{0,96},{8,104},{16,112},{24,120},{32,0},{40,8},{48,16},{56,24},{64... | collective-permute-start | bytes 393224 | tf_op jit(solution)/shard_map/ppermute | solution.py:29
  18.3 7.5 %collective-permute-start.6 = (bf16[256,256]{1,0:T(8,128)(2,1)S(1)}, bf16[256,256]{1,0:T(8,128)(2,1)S(1)}, u32[]{:S(2)}, u32[]{:S(2)}) collective-permute-start(bf16[256,256]{1,0:T(8,128)(2,1)S(1)} %slice.240), channel_id=1, source_target_pairs={{0,32},{8,40},{16,48},{24,56},{32,64},{40,72},{48,80},{56,88},{64,... | collective-permute-start | bytes 393224 | tf_op jit(solution)/shard_map/ppermute | solution.py:29
  21.9 25.2 %collective-permute-start.9 = (bf16[512,1024]{1,0:T(8,128)(2,1)S(1)}, bf16[512,1024]{1,0:T(8,128)(2,1)S(1)}, u32[]{:S(2)}, u32[]{:S(2)}) collective-permute-start(bf16[512,1024]{1,0:T(8,128)(2,1)S(1)} %get-tuple-element.55), channel_id=1, source_target_pairs={{0,32},{8,40},{16,48},{24,56},{32,64},{40,72},{48,80},{56,88},{64,... | collective-permute-start | bytes 3145736 | tf_op jit(solution)/shard_map/ppermute | solution.py:29
  23.4 23.7 %collective-permute-start.8 = (bf16[512,1024]{1,0:T(8,128)(2,1)S(1)}, bf16[512,1024]{1,0:T(8,128)(2,1)S(1)}, u32[]{:S(2)}, u32[]{:S(2)}) collective-permute-start(bf16[512,1024]{1,0:T(8,128)(2,1)S(1)} %get-tuple-element.55), channel_id=1, source_target_pairs={{0,96},{8,104},{16,112},{24,120},{32,0},{40,8},{48,16},{56,24},{64... | collective-permute-start | bytes 3145736 | tf_op jit(solution)/shard_map/ppermute | solution.py:29
  26.1 24.4 %collective-permute-start.13 = (bf16[512,1024]{1,0:T(8,128)(2,1)S(1)}, bf16[512,1024]{1,0:T(8,128)(2,1)S(1)}, u32[]{:S(2)}, u32[]{:S(2)}) collective-permute-start(bf16[512,1024]{1,0:T(8,128)(2,1)S(1)} %get-tuple-element.53), channel_id=1, source_target_pairs={{0,8},{8,16},{16,24},{24,0},{32,40},{40,48},{48,56},{56,32},{64,72... | collective-permute-start | bytes 3145736 | tf_op jit(solution)/shard_map/ppermute | solution.py:29
  26.5 24.1 %collective-permute-start.12 = (bf16[512,1024]{1,0:T(8,128)(2,1)S(1)}, bf16[512,1024]{1,0:T(8,128)(2,1)S(1)}, u32[]{:S(2)}, u32[]{:S(2)}) collective-permute-start(bf16[512,1024]{1,0:T(8,128)(2,1)S(1)} %get-tuple-element.53), channel_id=1, source_target_pairs={{0,24},{8,0},{16,8},{24,16},{32,56},{40,32},{48,40},{56,48},{64,88... | collective-permute-start | bytes 3145736 | tf_op jit(solution)/shard_map/ppermute | solution.py:29
  29.9 3.4 %copy-start.1 = (bf16[1024,4096]{1,0:T(8,128)(2,1)S(1)}, bf16[1024,4096]{1,0:T(8,128)(2,1)}, u32[]{:S(2)}) copy-start(bf16[1024,4096]{1,0:T(8,128)(2,1)} %rows_ref.1) | copy-start | bytes 25165828
  47.1 15.4 %collective-permute-start.10 = (bf16[256,1024]{1,0:T(8,128)(2,1)S(1)}, bf16[256,1024]{1,0:T(8,128)(2,1)S(1)}, u32[]{:S(2)}, u32[]{:S(2)}) collective-permute-start(bf16[256,1024]{1,0:T(8,128)(2,1)S(1)} %slice.242), channel_id=1, source_target_pairs={{0,32},{8,40},{16,48},{24,56},{32,64},{40,72},{48,80},{56,88},{64,... | collective-permute-start | bytes 1572872 | tf_op jit(solution)/shard_map/ppermute | solution.py:29
  47.2 15.8 %collective-permute-start.11 = (bf16[256,1024]{1,0:T(8,128)(2,1)S(1)}, bf16[256,1024]{1,0:T(8,128)(2,1)S(1)}, u32[]{:S(2)}, u32[]{:S(2)}) collective-permute-start(bf16[256,1024]{1,0:T(8,128)(2,1)S(1)} %slice.243), channel_id=1, source_target_pairs={{0,96},{8,104},{16,112},{24,120},{32,0},{40,8},{48,16},{56,24},{64... | collective-permute-start | bytes 1572872 | tf_op jit(solution)/shard_map/ppermute | solution.py:29
  50.5 12.4 %collective-permute-start.14 = (bf16[256,1024]{1,0:T(8,128)(2,1)S(1)}, bf16[256,1024]{1,0:T(8,128)(2,1)S(1)}, u32[]{:S(2)}, u32[]{:S(2)}) collective-permute-start(bf16[256,1024]{1,0:T(8,128)(2,1)S(1)} %slice.244), channel_id=1, source_target_pairs={{0,8},{8,16},{16,24},{24,0},{32,40},{40,48},{48,56},{56,32},{64,72... | collective-permute-start | bytes 1572872 | tf_op jit(solution)/shard_map/ppermute | solution.py:29
  50.6 14.0 %collective-permute-start.15 = (bf16[256,1024]{1,0:T(8,128)(2,1)S(1)}, bf16[256,1024]{1,0:T(8,128)(2,1)S(1)}, u32[]{:S(2)}, u32[]{:S(2)}) collective-permute-start(bf16[256,1024]{1,0:T(8,128)(2,1)S(1)} %slice.245), channel_id=1, source_target_pairs={{0,24},{8,0},{16,8},{24,16},{32,56},{40,32},{48,40},{56,48},{64,88... | collective-permute-start | bytes 1572872 | tf_op jit(solution)/shard_map/ppermute | solution.py:29
  132.4 16.1 %collective-permute-start.20 = (f16[2,528,256]{2,1,0:T(8,128)(2,1)S(1)}, f16[2,528,256]{2,1,0:T(8,128)(2,1)S(1)}, u32[]{:S(2)}, u32[]{:S(2)}) collective-permute-start(f16[2,528,256]{2,1,0:T(8,128)(2,1)S(1)} %get-tuple-element.69), channel_id=1, source_target_pairs={{0,32},{8,40},{16,48},{24,56},{32,64},{40,72},{48,80},{56,88},{64,... | collective-permute-start | bytes 1622024 | tf_op jit(solution)/shard_map/ppermute | solution.py:29
  133.0 15.6 %collective-permute-start.22 = (f16[2,528,256]{2,1,0:T(8,128)(2,1)S(1)}, f16[2,528,256]{2,1,0:T(8,128)(2,1)S(1)}, u32[]{:S(2)}, u32[]{:S(2)}) collective-permute-start(f16[2,528,256]{2,1,0:T(8,128)(2,1)S(1)} %get-tuple-element.68), channel_id=1, source_target_pairs={{0,96},{8,104},{16,112},{24,120},{32,0},{40,8},{48,16},{56,24},{64... | collective-permute-start | bytes 1622024 | tf_op jit(solution)/shard_map/ppermute | solution.py:29
  138.3 14.3 %collective-permute-start.18 = (f16[2,528,256]{2,1,0:T(8,128)(2,1)S(1)}, f16[2,528,256]{2,1,0:T(8,128)(2,1)S(1)}, u32[]{:S(2)}, u32[]{:S(2)}) collective-permute-start(f16[2,528,256]{2,1,0:T(8,128)(2,1)S(1)} %get-tuple-element.66), channel_id=1, source_target_pairs={{0,24},{8,0},{16,8},{24,16},{32,56},{40,32},{48,40},{56,48},{64,88... | collective-permute-start | bytes 1622024 | tf_op jit(solution)/shard_map/ppermute | solution.py:29
  139.6 14.3 %collective-permute-start.16 = (f16[2,528,256]{2,1,0:T(8,128)(2,1)S(1)}, f16[2,528,256]{2,1,0:T(8,128)(2,1)S(1)}, u32[]{:S(2)}, u32[]{:S(2)}) collective-permute-start(f16[2,528,256]{2,1,0:T(8,128)(2,1)S(1)} %get-tuple-element.67), channel_id=1, source_target_pairs={{0,8},{8,16},{16,24},{24,0},{32,40},{40,48},{48,56},{56,32},{64,72... | collective-permute-start | bytes 1622024 | tf_op jit(solution)/shard_map/ppermute | solution.py:29
  150.5 24.7 %collective-permute-start.23 = (f16[4,528,256]{2,1,0:T(8,128)(2,1)}, f16[4,528,256]{2,1,0:T(8,128)(2,1)}, u32[]{:S(2)}, u32[]{:S(2)}) collective-permute-start(f16[4,528,256]{2,1,0:T(8,128)(2,1)} %get-tuple-element.63), channel_id=1, source_target_pairs={{0,96},{8,104},{16,112},{24,120},{32,0},{40,8},{48,16},{56,24},{64... | collective-permute-start | bytes 3244040 | tf_op jit(solution)/shard_map/ppermute | solution.py:29
  152.5 25.4 %collective-permute-start.21 = (f16[4,528,256]{2,1,0:T(8,128)(2,1)S(1)}, f16[4,528,256]{2,1,0:T(8,128)(2,1)}, u32[]{:S(2)}, u32[]{:S(2)}) collective-permute-start(f16[4,528,256]{2,1,0:T(8,128)(2,1)S(1)} %get-tuple-element.62), channel_id=1, source_target_pairs={{0,32},{8,40},{16,48},{24,56},{32,64},{40,72},{48,80},{56,88},{64,... | collective-permute-start | bytes 3244040 | tf_op jit(solution)/shard_map/ppermute | solution.py:29
  156.0 25.3 %collective-permute-start.17 = (f16[4,528,256]{2,1,0:T(8,128)(2,1)}, f16[4,528,256]{2,1,0:T(8,128)(2,1)}, u32[]{:S(2)}, u32[]{:S(2)}) collective-permute-start(f16[4,528,256]{2,1,0:T(8,128)(2,1)} %get-tuple-element.65), channel_id=1, source_target_pairs={{0,8},{8,16},{16,24},{24,0},{32,40},{40,48},{48,56},{56,32},{64,72... | collective-permute-start | bytes 3244040 | tf_op jit(solution)/shard_map/ppermute | solution.py:29
  156.0 25.3 %collective-permute-start.19 = (f16[4,528,256]{2,1,0:T(8,128)(2,1)}, f16[4,528,256]{2,1,0:T(8,128)(2,1)}, u32[]{:S(2)}, u32[]{:S(2)}) collective-permute-start(f16[4,528,256]{2,1,0:T(8,128)(2,1)} %get-tuple-element.64), channel_id=1, source_target_pairs={{0,24},{8,0},{16,8},{24,16},{32,56},{40,32},{48,40},{56,48},{64,88... | collective-permute-start | bytes 3244040 | tf_op jit(solution)/shard_map/ppermute | solution.py:29
  163.4 2.0 copy-start
  181.3 9.9 %collective-permute-start.29 = (f16[528,256]{1,0:T(8,128)(2,1)S(1)}, f16[528,256]{1,0:T(8,128)(2,1)S(1)}, u32[]{:S(2)}, u32[]{:S(2)}) collective-permute-start(f16[528,256]{1,0:T(8,128)(2,1)S(1)} %get-tuple-element.41), channel_id=1, source_target_pairs={{0,16},{8,24},{16,0},{24,8},{32,48},{40,56},{48,32},{56,40},{64,80... | collective-permute-start | bytes 811016 | tf_op jit(solution)/shard_map/ppermute | solution.py:29
  182.8 11.4 %collective-permute-start.28 = (f16[528,256]{1,0:T(8,128)(2,1)S(1)}, f16[528,256]{1,0:T(8,128)(2,1)S(1)}, u32[]{:S(2)}, u32[]{:S(2)}) collective-permute-start(f16[528,256]{1,0:T(8,128)(2,1)S(1)} %get-tuple-element.40), channel_id=1, source_target_pairs={{0,24},{8,0},{16,8},{24,16},{32,56},{40,32},{48,40},{56,48},{64,88... | collective-permute-start | bytes 811016 | tf_op jit(solution)/shard_map/ppermute | solution.py:29
  184.3 9.9 %collective-permute-start.27 = (f16[528,256]{1,0:T(8,128)(2,1)S(1)}, f16[528,256]{1,0:T(8,128)(2,1)S(1)}, u32[]{:S(2)}, u32[]{:S(2)}) collective-permute-start(f16[528,256]{1,0:T(8,128)(2,1)S(1)} %get-tuple-element.39), channel_id=1, source_target_pairs={{0,8},{8,16},{16,24},{24,0},{32,40},{40,48},{48,56},{56,32},{64,72... | collective-permute-start | bytes 811016 | tf_op jit(solution)/shard_map/ppermute | solution.py:29
  187.5 8.9 %collective-permute-start.24 = (f16[528,256]{1,0:T(8,128)(2,1)S(1)}, f16[528,256]{1,0:T(8,128)(2,1)S(1)}, u32[]{:S(2)}, u32[]{:S(2)}) collective-permute-start(f16[528,256]{1,0:T(8,128)(2,1)S(1)} %get-tuple-element.58), channel_id=1, source_target_pairs={{0,32},{8,40},{16,48},{24,56},{32,64},{40,72},{48,80},{56,88},{64,... | collective-permute-start | bytes 811016 | tf_op jit(solution)/shard_map/ppermute | solution.py:29
  187.5 10.9 %collective-permute-start.25 = (f16[528,256]{1,0:T(8,128)(2,1)S(1)}, f16[528,256]{1,0:T(8,128)(2,1)S(1)}, u32[]{:S(2)}, u32[]{:S(2)}) collective-permute-start(f16[528,256]{1,0:T(8,128)(2,1)S(1)} %get-tuple-element.57), channel_id=1, source_target_pairs={{0,96},{8,104},{16,112},{24,120},{32,0},{40,8},{48,16},{56,24},{64... | collective-permute-start | bytes 811016 | tf_op jit(solution)/shard_map/ppermute | solution.py:29
  191.3 8.0 %collective-permute-start.26 = (f16[528,256]{1,0:T(8,128)(2,1)S(1)}, f16[528,256]{1,0:T(8,128)(2,1)S(1)}, u32[]{:S(2)}, u32[]{:S(2)}) collective-permute-start(f16[528,256]{1,0:T(8,128)(2,1)S(1)} %get-tuple-element.56), channel_id=1, source_target_pairs={{0,64},{8,72},{16,80},{24,88},{32,96},{40,104},{48,112},{56,120},{... | collective-permute-start | bytes 811016 | tf_op jit(solution)/shard_map/ppermute | solution.py:29

commit v2 on v1

--- a/solution.py
+++ b/solution.py
@@ -105,7 +105,6 @@
 
 
 CHUNK = 128
-FULL = lax.Precision.HIGHEST
 
 
 def _chunks(refs):
@@ -126,11 +125,8 @@
     return sum(value[:, i : i + CHUNK] for i in range(0, value.shape[1], CHUNK))
 
 
-def _lane_sums(folded, copies):
-    ones = jnp.ones((copies, CHUNK), jnp.float32)
-    return lax.dot_general(
-        ones, folded, (((1,), (1,)), ((), ())), precision=FULL, preferred_element_type=jnp.float32
-    )
+def _lane_sums(folded):
+    return jnp.sum(folded.T, 0, keepdims=True)
 
 
 def _row_sums_kernel(target, a_ref, b_ref, column_ref, out_ref, scale_ref):
@@ -147,7 +143,8 @@
 def _column_sums_kernel(a_ref, b_ref, row_ref, out_ref):
     scale = 1.0 / jnp.sum(row_ref[...], 0)
     for ref, cut, whole in _chunks((a_ref, b_ref)):
-        out_ref[:, 0, whole] = _lane_sums(_fold(ref[cut, :] * scale), out_ref.shape[0])
+        sums = _lane_sums(_fold(ref[cut, :] * scale))
+        out_ref[:, 0, whole] = jnp.broadcast_to(sums, (out_ref.shape[0], CHUNK))
 
 
 def _shares_kernel(target, a_ref, b_ref, column_ref, row_ref, shares_ref, mass_ref, scale_ref):
@@ -159,7 +156,7 @@
         scale = _column_chunk(scale_ref, whole, ref.shape[1]) * row_scale
         shares = (ref[cut, :] * scale).astype(jnp.bfloat16)
         shares_ref[whole, :] = shares
-        mass = _lane_sums(_fold(shares.astype(jnp.float32)), 8)
+        mass = _lane_sums(_fold(shares.astype(jnp.float32)))
         half, place = divmod(whole.start, shares_ref.shape[0] // halves)
         row, lane = divmod(place, width)
         mass_ref[half, row, lane : lane + CHUNK] = mass[0]

time: 202 us -> 200 us (0.990)
  no operation moved by 1% of the time
where the time goes in v2:
time: 200 us
  blocking collectives  57.5 us (29%)
  starting transfers between devices  46.3 us (23%)
  Pallas kernels  33.3 us (17%)
  waiting for transfers between devices  30 us (15%)
  other arithmetic  17.2 us (9%)
  local copies, waits for them, and re-layouts  9.34 us (5%)
  matrix products  5.18 us (3%)
    all_to_all x6, blocking collectives, _exchange(): return lax.all_to_all(copies, axis, 0, 0)  57.5 us
    ppermute x30, starting transfers between devices, _send(): return lax.ppermute(value, 'dp', axis(step))  46.3 us
    ppermute x30, waiting for transfers between devices, _send(): return lax.ppermute(value, 'dp', axis(step))  30 us
    pallas_call x5, Pallas kernels, _part(): pl.pallas_call(functools.partial(_part_kernel, halves), in_specs=[pl.Bloc...  16.8 us
    convert_element_type x6, other arithmetic, _pack(): return (value * PACK).astype(jnp.float16)  8.83 us
    unnamed x11, local copies, waits for them, and re-layouts  7.97 us
    pallas_call x2, Pallas kernels, _near_scores(): pl.pallas_call(_near_scores_kernel, grid=(SIDE,), in_specs=[tiles, panel,...  7.19 us
    pallas_call x1, Pallas kernels, _reorder(): pl.pallas_call(_reorder_kernel, grid_spec=pltpu.PrefetchScalarGridSpec(nu...  6.45 us
  transfers between devices with their start and end apart: 30, of which 14 were waited for; matrix products, arithmetic and copies ran while one was open for 10% of the time, Pallas kernels for 14%

profile of v2, /device:TPU:0, one launch (start us, length us, event | category | flops | bytes accessed | tf_op | source)
XLA Modules:
  0.0 199.9 jit_solution(14125815634152890172)
XLA Ops:
  9.3 2.4 %collective-permute-done = bf16[512,256]{1,0:T(8,128)(2,1)S(1)} collective-permute-done((bf16[512,256]{1,0:T(8,128)(2,1)S(1)}, bf16[512,256]{1,0:T(8,128)(2,1)S(1)}, u32[]{:S(2)}, u32[]{:S(2)}) %collective-permute-start) | collective-permute-done | bytes 262176 | tf_op jit(solution)/shard_map/ppermute | solution.py:29
  11.7 3.6 %collective-permute-start.3 = (bf16[256,256]{1,0:T(8,128)(2,1)S(1)}, bf16[256,256]{1,0:T(8,128)(2,1)S(1)}, u32[]{:S(2)}, u32[]{:S(2)}) collective-permute-start(bf16[256,256]{1,0:T(8,128)(2,1)S(1)} %slice.239), channel_id=1, source_target_pairs={{0,24},{8,0},{16,8},{24,16},{32,56},{40,32},{48,40},{56,48},{64,88... | collective-permute-start | bytes 393224 | tf_op jit(solution)/shard_map/ppermute | solution.py:29
  15.5 2.8 %collective-permute-start.7 = (bf16[256,256]{1,0:T(8,128)(2,1)S(1)}, bf16[256,256]{1,0:T(8,128)(2,1)S(1)}, u32[]{:S(2)}, u32[]{:S(2)}) collective-permute-start(bf16[256,256]{1,0:T(8,128)(2,1)S(1)} %slice.241), channel_id=1, source_target_pairs={{0,96},{8,104},{16,112},{24,120},{32,0},{40,8},{48,16},{56,24},{64... | collective-permute-start | bytes 393224 | tf_op jit(solution)/shard_map/ppermute | solution.py:29
  18.4 3.2 %collective-permute-done.2 = bf16[256,256]{1,0:T(8,128)(2,1)S(1)} collective-permute-done((bf16[256,256]{1,0:T(8,128)(2,1)S(1)}, bf16[256,256]{1,0:T(8,128)(2,1)S(1)}, u32[]{:S(2)}, u32[]{:S(2)}) %collective-permute-start.2) | collective-permute-done | bytes 131104 | tf_op jit(solution)/shard_map/ppermute | solution.py:29
  26.5 3.2 %collective-permute-start.12 = (bf16[512,1024]{1,0:T(8,128)(2,1)S(1)}, bf16[512,1024]{1,0:T(8,128)(2,1)S(1)}, u32[]{:S(2)}, u32[]{:S(2)}) collective-permute-start(bf16[512,1024]{1,0:T(8,128)(2,1)S(1)} %get-tuple-element.53), channel_id=1, source_target_pairs={{0,24},{8,0},{16,8},{24,16},{32,56},{40,32},{48,40},{56,48},{64,88... | collective-permute-start | bytes 3145736 | tf_op jit(solution)/shard_map/ppermute | solution.py:29
  29.9 3.4 %copy-done.1 = bf16[1024,4096]{1,0:T(8,128)(2,1)S(1)} copy-done((bf16[1024,4096]{1,0:T(8,128)(2,1)S(1)}, bf16[1024,4096]{1,0:T(8,128)(2,1)}, u32[]{:S(2)}) %copy-start.1) | copy-done | bytes 8388632
  33.3 6.5 %shard_map.41 = (bf16[1024,4096]{1,0:T(8,128)(2,1)S(1)}, bf16[1024,4096]{1,0:T(8,128)(2,1)S(1)}, bf16[16,1024,256]{2,1,0:T(8,128)(2,1)S(1)}) custom-call(s32[2]{0:T(128)S(1)} %pad_add_fusion.place_ref, bf16[1024,4096]{1,0:T(8,128)(2,1)S(1)} %copy-done.1), custom_call_target="tpu_custom_call" | custom-call | flops 12582912 | bytes 33554432 | tf_op jit(solution)/shard_map/pallas_call | solution.py:296
  42.3 4.7 %collective-permute-done.9.before_ref = bf16[512,1024]{1,0:T(8,128)(2,1)S(1)} collective-permute-done((bf16[512,1024]{1,0:T(8,128)(2,1)S(1)}, bf16[512,1024]{1,0:T(8,128)(2,1)S(1)}, u32[]{:S(2)}, u32[]{:S(2)}) %collective-permute-start.9) | collective-permute-done | bytes 1048608 | tf_op jit(solution)/shard_map/ppermute | solution.py:29
  47.2 3.3 %collective-permute-start.11 = (bf16[256,1024]{1,0:T(8,128)(2,1)S(1)}, bf16[256,1024]{1,0:T(8,128)(2,1)S(1)}, u32[]{:S(2)}, u32[]{:S(2)}) collective-permute-start(bf16[256,1024]{1,0:T(8,128)(2,1)S(1)} %slice.243), channel_id=1, source_target_pairs={{0,96},{8,104},{16,112},{24,120},{32,0},{40,8},{48,16},{56,24},{64... | collective-permute-start | bytes 1572872 | tf_op jit(solution)/shard_map/ppermute | solution.py:29
  50.6 3.5 %collective-permute-start.15 = (bf16[256,1024]{1,0:T(8,128)(2,1)S(1)}, bf16[256,1024]{1,0:T(8,128)(2,1)S(1)}, u32[]{:S(2)}, u32[]{:S(2)}) collective-permute-start(bf16[256,1024]{1,0:T(8,128)(2,1)S(1)} %slice.245), channel_id=1, source_target_pairs={{0,24},{8,0},{16,8},{24,16},{32,56},{40,32},{48,40},{56,48},{64,88... | collective-permute-start | bytes 1572872 | tf_op jit(solution)/shard_map/ppermute | solution.py:29
  54.7 3.6 %shard_map.42 = f32[512,1024]{1,0:T(8,128)S(1)} custom-call(f32[512,1024]{1,0:T(8,128)S(1)} %fusion.14.total_ref, bf16[512,1024]{1,0:T(8,128)(2,1)S(1)} %collective-permute-done.8.after_ref, bf16[512,1024]{1,0:T(8,128)(2,1)S(1)} %collective-permute-done.9.before_ref, bf16[1024,4096]{1,0:T(8,128)(2,1)S(1)} %get-tuple-element.25.rows_1_ref.rows_3_ref, ...), custom_call_target="tpu_custom_call" | custom-call | flops 2147483648 | bytes 10485760 | tf_op jit(solution)/shard_map/pallas_call | solution.py:67
  58.8 3.6 %shard_map.43 = f32[512,1024]{1,0:T(8,128)S(1)} custom-call(f32[512,1024]{1,0:T(8,128)S(1)} %fusion.10.total_ref, bf16[512,1024]{1,0:T(8,128)(2,1)S(1)} %collective-permute-done.12.after_ref, bf16[512,1024]{1,0:T(8,128)(2,1)S(1)} %collective-permute-done.13.before_ref, bf16[1024,4096]{1,0:T(8,128)(2,1)S(1)} %get-tuple-element.26.rows_1_ref.rows_3_ref, ...), custom_call_target="tpu_custom_call" | custom-call | flops 2147483648 | bytes 10485760 | tf_op jit(solution)/shard_map/pallas_call | solution.py:67
  67.6 10.4 %all_to_all.30.column_ref = f32[16,1,1024]{2,1,0:T(1,128)S(1)} all-to-all(f32[16,1,1024]{2,1,0:T(1,128)S(1)} %broadcast_in_dim.2), channel_id=1, replica_groups=mesh['dp'=16,'cent'=8] {'dp'}, dimensions={0} | all-to-all | bytes 131072 | tf_op jit(solution)/shard_map/all_to_all | solution.py:182
  78.4 9.7 %all_to_all.31.row_ref = f32[8,1,1024]{2,1,0:T(1,128)S(1)} all-to-all(f32[8,1,1024]{2,1,0:T(1,128)S(1)} %shard_map.44), channel_id=1, replica_groups=mesh['dp'=16,'cent'=8] {'cent'}, dimensions={0} | all-to-all | bytes 65536 | tf_op jit(solution)/shard_map/all_to_all | solution.py:182
  88.5 10.9 %all_to_all.32.column_ref = f32[16,1,1024]{2,1,0:T(1,128)S(1)} all-to-all(f32[16,1,1024]{2,1,0:T(1,128)S(1)} %shard_map.45), channel_id=1, replica_groups=mesh['dp'=16,'cent'=8] {'dp'}, dimensions={0} | all-to-all | bytes 131072 | tf_op jit(solution)/shard_map/all_to_all | solution.py:182
  99.8 7.8 %all_to_all.33.row_ref = f32[8,1,1024]{2,1,0:T(1,128)S(1)} all-to-all(f32[8,1,1024]{2,1,0:T(1,128)S(1)} %shard_map.46), channel_id=1, replica_groups=mesh['dp'=16,'cent'=8] {'cent'}, dimensions={0} | all-to-all | bytes 65536 | tf_op jit(solution)/shard_map/all_to_all | solution.py:182
  108.0 10.9 %all_to_all.34.column_ref = f32[16,1,1024]{2,1,0:T(1,128)S(1)} all-to-all(f32[16,1,1024]{2,1,0:T(1,128)S(1)} %shard_map.47), channel_id=1, replica_groups=mesh['dp'=16,'cent'=8] {'dp'}, dimensions={0} | all-to-all | bytes 131072 | tf_op jit(solution)/shard_map/all_to_all | solution.py:182
  119.3 7.8 %all_to_all.35.row_ref = f32[8,1,1024]{2,1,0:T(1,128)S(1)} all-to-all(f32[8,1,1024]{2,1,0:T(1,128)S(1)} %shard_map.48), channel_id=1, replica_groups=mesh['dp'=16,'cent'=8] {'cent'}, dimensions={0} | all-to-all | bytes 65536 | tf_op jit(solution)/shard_map/all_to_all | solution.py:182
  128.0 2.3 %shard_map.50 = f32[4,528,256]{2,1,0:T(8,128)S(1)} custom-call(s32[4]{0:T(128)S(1)} %get-tuple-element.30.slots_ref, bf16[1024,1024]{1,0:T(8,128)(2,1)S(1)} %get-tuple-element.34.shares_ref, f32[2,16,256]{2,1,0:T(8,128)S(1)} %get-tuple-element.31.mass_ref, bf16[16,1024,256]{2,1,0:T(8,128)(2,1)S(1)} %get-tuple-element.32.rows_ref), custom_call_target="tpu_custom_call" | custom-call | flops 2147483648 | bytes 4194304 | tf_op jit(solution)/shard_map/pallas_call | solution.py:206
  131.2 2.7 %collective-permute-start.22 = (f16[2,528,256]{2,1,0:T(8,128)(2,1)S(1)}, f16[2,528,256]{2,1,0:T(8,128)(2,1)S(1)}, u32[]{:S(2)}, u32[]{:S(2)}) collective-permute-start(f16[2,528,256]{2,1,0:T(8,128)(2,1)S(1)} %get-tuple-element.68), channel_id=1, source_target_pairs={{0,96},{8,104},{16,112},{24,120},{32,0},{40,8},{48,16},{56,24},{64... | collective-permute-start | bytes 1622024 | tf_op jit(solution)/shard_map/ppermute | solution.py:29
  133.9 2.3 %shard_map.51 = f32[4,528,256]{2,1,0:T(8,128)S(1)} custom-call(s32[4]{0:T(128)S(1)} %get-tuple-element.33.slots_ref, bf16[1024,1024]{1,0:T(8,128)(2,1)S(1)} %get-tuple-element.34.shares_ref, f32[2,16,256]{2,1,0:T(8,128)S(1)} %get-tuple-element.31.mass_ref, bf16[16,1024,256]{2,1,0:T(8,128)(2,1)S(1)} %get-tuple-element.32.rows_ref), custom_call_target="tpu_custom_call" | custom-call | flops 2147483648 | bytes 4194304 | tf_op jit(solution)/shard_map/pallas_call | solution.py:206
  138.5 4.1 %shard_map.53 = f32[8,528,256]{2,1,0:T(8,128)S(1)} custom-call(s32[8]{0:T(128)S(1)} %pad_add_fusion.2.slots_ref, bf16[1024,1024]{1,0:T(8,128)(2,1)S(1)} %get-tuple-element.34.shares_ref, f32[2,16,256]{2,1,0:T(8,128)S(1)} %get-tuple-element.31.mass_ref, bf16[16,1024,256]{2,1,0:T(8,128)(2,1)S(1)} %get-tuple-element.32.rows_ref), custom_call_target="tpu_custom_call" | custom-call | flops 1000 | bytes 1 | tf_op jit(solution)/shard_map/pallas_call | solution.py:206
  142.6 4.1 %shard_map.54 = f32[8,528,256]{2,1,0:T(8,128)S(1)} custom-call(s32[8]{0:T(128)S(1)} %pad_add_fusion.1.slots_ref, bf16[1024,1024]{1,0:T(8,128)(2,1)S(1)} %get-tuple-element.34.shares_ref, f32[2,16,256]{2,1,0:T(8,128)S(1)} %get-tuple-element.31.mass_ref, bf16[16,1024,256]{2,1,0:T(8,128)(2,1)S(1)} %get-tuple-element.32.rows_ref), custom_call_target="tpu_custom_call" | custom-call | flops 1000 | bytes 1 | tf_op jit(solution)/shard_map/pallas_call | solution.py:206
  154.2 3.2 %collective-permute-start.19 = (f16[4,528,256]{2,1,0:T(8,128)(2,1)}, f16[4,528,256]{2,1,0:T(8,128)(2,1)}, u32[]{:S(2)}, u32[]{:S(2)}) collective-permute-start(f16[4,528,256]{2,1,0:T(8,128)(2,1)} %get-tuple-element.64), channel_id=1, source_target_pairs={{0,24},{8,0},{16,8},{24,16},{32,56},{40,32},{48,40},{56,48},{64,88... | collective-permute-start | bytes 3244040 | tf_op jit(solution)/shard_map/ppermute | solution.py:29
  157.5 4.1 %shard_map.52 = f32[8,528,256]{2,1,0:T(8,128)S(1)} custom-call(s32[8]{0:T(128)S(1)} %pad_add_fusion.3.slots_ref, bf16[1024,1024]{1,0:T(8,128)(2,1)S(1)} %get-tuple-element.34.shares_ref, f32[2,16,256]{2,1,0:T(8,128)S(1)} %get-tuple-element.31.mass_ref, bf16[16,1024,256]{2,1,0:T(8,128)(2,1)S(1)} %get-tuple-element.32.rows_ref), custom_call_target="tpu_custom_call" | custom-call | flops 1000 | bytes 1 | tf_op jit(solution)/shard_map/pallas_call | solution.py:206
  163.6 2.5 %copy.4 = bf16[1024,1024]{1,0:T(8,128)(2,1)} copy(bf16[1024,1024]{0,1:T(8,128)(2,1)S(1)} %bitcast.57) | data formatting | bytes 4194304
  166.1 7.3 %collective-permute-done.23 = f16[4,528,256]{2,1,0:T(8,128)(2,1)} collective-permute-done((f16[4,528,256]{2,1,0:T(8,128)(2,1)}, f16[4,528,256]{2,1,0:T(8,128)(2,1)}, u32[]{:S(2)}, u32[]{:S(2)}) %collective-permute-start.23) | collective-permute-done | bytes 1081376 | tf_op jit(solution)/shard_map/ppermute | solution.py:29
  173.4 2.6 %collective-permute-done.21 = f16[4,528,256]{2,1,0:T(8,128)(2,1)} collective-permute-done((f16[4,528,256]{2,1,0:T(8,128)(2,1)S(1)}, f16[4,528,256]{2,1,0:T(8,128)(2,1)}, u32[]{:S(2)}, u32[]{:S(2)}) %collective-permute-start.21) | collective-permute-done | bytes 1081376 | tf_op jit(solution)/shard_map/ppermute | solution.py:29
  176.0 2.3 %fusion.53 = (f16[528,256]{1,0:T(8,128)(2,1)S(1)}, f16[528,256]{1,0:T(8,128)(2,1)S(1)}, f16[528,256]{1,0:T(8,128)(2,1)S(1)}) fusion(f32[8,528,256]{2,1,0:T(8,128)} %copy-done, f16[4,528,256]{2,1,0:T(8,128)(2,1)} %collective-permute-done.23, f16[4,528,256]{2,1,0:T(8,128)(2,1)} %collective-permute-done.21), kind=kLoop, calls=%fused_computation.88 | loop fusion | flops 3244032 | bytes 4055040 | tf_op jit(solution)/shard_map/convert_element_type | solution.py:100
  183.3 2.3 %fusion.55 = (f16[528,256]{1,0:T(8,128)(2,1)S(1)}, f16[528,256]{1,0:T(8,128)(2,1)S(1)}, f16[528,256]{1,0:T(8,128)(2,1)S(1)}) fusion(f32[8,528,256]{2,1,0:T(8,128)} %copy-done, f16[4,528,256]{2,1,0:T(8,128)(2,1)} %collective-permute-done.19, f16[4,528,256]{2,1,0:T(8,128)(2,1)} %collective-permute-done.17), kind=kLoop, calls=%fused_computation.90 | loop fusion | flops 3244032 | bytes 4055040 | tf_op jit(solution)/shard_map/convert_element_type | solution.py:100
  185.7 3.2 %collective-permute-start.25 = (f16[528,256]{1,0:T(8,128)(2,1)S(1)}, f16[528,256]{1,0:T(8,128)(2,1)S(1)}, u32[]{:S(2)}, u32[]{:S(2)}) collective-permute-start(f16[528,256]{1,0:T(8,128)(2,1)S(1)} %get-tuple-element.57), channel_id=1, source_target_pairs={{0,96},{8,104},{16,112},{24,120},{32,0},{40,8},{48,16},{56,24},{64... | collective-permute-start | bytes 811016 | tf_op jit(solution)/shard_map/ppermute | solution.py:29
  190.2 2.2 %collective-permute-done.28 = f16[528,256]{1,0:T(8,128)(2,1)S(1)} collective-permute-done((f16[528,256]{1,0:T(8,128)(2,1)S(1)}, f16[528,256]{1,0:T(8,128)(2,1)S(1)}, u32[]{:S(2)}, u32[]{:S(2)}) %collective-permute-start.28) | collective-permute-done | bytes 270368 | tf_op jit(solution)/shard_map/ppermute | solution.py:29
  (111 shorter events, 52.5 us)
Async XLA Ops:
  1.7 13.6 %collective-permute-start.1 = (bf16[512,256]{1,0:T(8,128)(2,1)S(1)}, bf16[512,256]{1,0:T(8,128)(2,1)S(1)}, u32[]{:S(2)}, u32[]{:S(2)}) collective-permute-start(bf16[512,256]{1,0:T(8,128)(2,1)S(1)} %get-tuple-element.71), channel_id=1, source_target_pairs={{0,8},{8,16},{16,24},{24,0},{32,40},{40,48},{48,56},{56,32},{64,72... | collective-permute-start | bytes 786440 | tf_op jit(solution)/shard_map/ppermute | solution.py:29
  3.8 7.9 %collective-permute-start = (bf16[512,256]{1,0:T(8,128)(2,1)S(1)}, bf16[512,256]{1,0:T(8,128)(2,1)S(1)}, u32[]{:S(2)}, u32[]{:S(2)}) collective-permute-start(bf16[512,256]{1,0:T(8,128)(2,1)S(1)} %get-tuple-element.71), channel_id=1, source_target_pairs={{0,24},{8,0},{16,8},{24,16},{32,56},{40,32},{48,40},{56,48},{64,88... | collective-permute-start | bytes 786440 | tf_op jit(solution)/shard_map/ppermute | solution.py:29
  6.0 12.3 %collective-permute-start.5 = (bf16[512,256]{1,0:T(8,128)(2,1)S(1)}, bf16[512,256]{1,0:T(8,128)(2,1)S(1)}, u32[]{:S(2)}, u32[]{:S(2)}) collective-permute-start(bf16[512,256]{1,0:T(8,128)(2,1)S(1)} %get-tuple-element.70), channel_id=1, source_target_pairs={{0,32},{8,40},{16,48},{24,56},{32,64},{40,72},{48,80},{56,88},{64,... | collective-permute-start | bytes 786440 | tf_op jit(solution)/shard_map/ppermute | solution.py:29
  7.5 8.0 %collective-permute-start.4 = (bf16[512,256]{1,0:T(8,128)(2,1)S(1)}, bf16[512,256]{1,0:T(8,128)(2,1)S(1)}, u32[]{:S(2)}, u32[]{:S(2)}) collective-permute-start(bf16[512,256]{1,0:T(8,128)(2,1)S(1)} %get-tuple-element.70), channel_id=1, source_target_pairs={{0,96},{8,104},{16,112},{24,120},{32,0},{40,8},{48,16},{56,24},{64... | collective-permute-start | bytes 786440 | tf_op jit(solution)/shard_map/ppermute | solution.py:29
  11.7 6.7 %collective-permute-start.3 = (bf16[256,256]{1,0:T(8,128)(2,1)S(1)}, bf16[256,256]{1,0:T(8,128)(2,1)S(1)}, u32[]{:S(2)}, u32[]{:S(2)}) collective-permute-start(bf16[256,256]{1,0:T(8,128)(2,1)S(1)} %slice.239), channel_id=1, source_target_pairs={{0,24},{8,0},{16,8},{24,16},{32,56},{40,32},{48,40},{56,48},{64,88... | collective-permute-start | bytes 393224 | tf_op jit(solution)/shard_map/ppermute | solution.py:29
  15.3 6.2 %collective-permute-start.2 = (bf16[256,256]{1,0:T(8,128)(2,1)S(1)}, bf16[256,256]{1,0:T(8,128)(2,1)S(1)}, u32[]{:S(2)}, u32[]{:S(2)}) collective-permute-start(bf16[256,256]{1,0:T(8,128)(2,1)S(1)} %slice.238), channel_id=1, source_target_pairs={{0,8},{8,16},{16,24},{24,0},{32,40},{40,48},{48,56},{56,32},{64,72... | collective-permute-start | bytes 393224 | tf_op jit(solution)/shard_map/ppermute | solution.py:29
  15.5 9.7 %collective-permute-start.7 = (bf16[256,256]{1,0:T(8,128)(2,1)S(1)}, bf16[256,256]{1,0:T(8,128)(2,1)S(1)}, u32[]{:S(2)}, u32[]{:S(2)}) collective-permute-start(bf16[256,256]{1,0:T(8,128)(2,1)S(1)} %slice.241), channel_id=1, source_target_pairs={{0,96},{8,104},{16,112},{24,120},{32,0},{40,8},{48,16},{56,24},{64... | collective-permute-start | bytes 393224 | tf_op jit(solution)/shard_map/ppermute | solution.py:29
  18.3 7.5 %collective-permute-start.6 = (bf16[256,256]{1,0:T(8,128)(2,1)S(1)}, bf16[256,256]{1,0:T(8,128)(2,1)S(1)}, u32[]{:S(2)}, u32[]{:S(2)}) collective-permute-start(bf16[256,256]{1,0:T(8,128)(2,1)S(1)} %slice.240), channel_id=1, source_target_pairs={{0,32},{8,40},{16,48},{24,56},{32,64},{40,72},{48,80},{56,88},{64,... | collective-permute-start | bytes 393224 | tf_op jit(solution)/shard_map/ppermute | solution.py:29
  21.9 25.2 %collective-permute-start.9 = (bf16[512,1024]{1,0:T(8,128)(2,1)S(1)}, bf16[512,1024]{1,0:T(8,128)(2,1)S(1)}, u32[]{:S(2)}, u32[]{:S(2)}) collective-permute-start(bf16[512,1024]{1,0:T(8,128)(2,1)S(1)} %get-tuple-element.55), channel_id=1, source_target_pairs={{0,32},{8,40},{16,48},{24,56},{32,64},{40,72},{48,80},{56,88},{64,... | collective-permute-start | bytes 3145736 | tf_op jit(solution)/shard_map/ppermute | solution.py:29
  23.4 23.7 %collective-permute-start.8 = (bf16[512,1024]{1,0:T(8,128)(2,1)S(1)}, bf16[512,1024]{1,0:T(8,128)(2,1)S(1)}, u32[]{:S(2)}, u32[]{:S(2)}) collective-permute-start(bf16[512,1024]{1,0:T(8,128)(2,1)S(1)} %get-tuple-element.55), channel_id=1, source_target_pairs={{0,96},{8,104},{16,112},{24,120},{32,0},{40,8},{48,16},{56,24},{64... | collective-permute-start | bytes 3145736 | tf_op jit(solution)/shard_map/ppermute | solution.py:29
  26.1 24.4 %collective-permute-start.13 = (bf16[512,1024]{1,0:T(8,128)(2,1)S(1)}, bf16[512,1024]{1,0:T(8,128)(2,1)S(1)}, u32[]{:S(2)}, u32[]{:S(2)}) collective-permute-start(bf16[512,1024]{1,0:T(8,128)(2,1)S(1)} %get-tuple-element.53), channel_id=1, source_target_pairs={{0,8},{8,16},{16,24},{24,0},{32,40},{40,48},{48,56},{56,32},{64,72... | collective-permute-start | bytes 3145736 | tf_op jit(solution)/shard_map/ppermute | solution.py:29
  26.5 24.1 %collective-permute-start.12 = (bf16[512,1024]{1,0:T(8,128)(2,1)S(1)}, bf16[512,1024]{1,0:T(8,128)(2,1)S(1)}, u32[]{:S(2)}, u32[]{:S(2)}) collective-permute-start(bf16[512,1024]{1,0:T(8,128)(2,1)S(1)} %get-tuple-element.53), channel_id=1, source_target_pairs={{0,24},{8,0},{16,8},{24,16},{32,56},{40,32},{48,40},{56,48},{64,88... | collective-permute-start | bytes 3145736 | tf_op jit(solution)/shard_map/ppermute | solution.py:29
  29.9 3.4 %copy-start.1 = (bf16[1024,4096]{1,0:T(8,128)(2,1)S(1)}, bf16[1024,4096]{1,0:T(8,128)(2,1)}, u32[]{:S(2)}) copy-start(bf16[1024,4096]{1,0:T(8,128)(2,1)} %rows_ref.1) | copy-start | bytes 25165828
  47.1 15.4 %collective-permute-start.10 = (bf16[256,1024]{1,0:T(8,128)(2,1)S(1)}, bf16[256,1024]{1,0:T(8,128)(2,1)S(1)}, u32[]{:S(2)}, u32[]{:S(2)}) collective-permute-start(bf16[256,1024]{1,0:T(8,128)(2,1)S(1)} %slice.242), channel_id=1, source_target_pairs={{0,32},{8,40},{16,48},{24,56},{32,64},{40,72},{48,80},{56,88},{64,... | collective-permute-start | bytes 1572872 | tf_op jit(solution)/shard_map/ppermute | solution.py:29
  47.2 15.8 %collective-permute-start.11 = (bf16[256,1024]{1,0:T(8,128)(2,1)S(1)}, bf16[256,1024]{1,0:T(8,128)(2,1)S(1)}, u32[]{:S(2)}, u32[]{:S(2)}) collective-permute-start(bf16[256,1024]{1,0:T(8,128)(2,1)S(1)} %slice.243), channel_id=1, source_target_pairs={{0,96},{8,104},{16,112},{24,120},{32,0},{40,8},{48,16},{56,24},{64... | collective-permute-start | bytes 1572872 | tf_op jit(solution)/shard_map/ppermute | solution.py:29
  50.5 12.4 %collective-permute-start.14 = (bf16[256,1024]{1,0:T(8,128)(2,1)S(1)}, bf16[256,1024]{1,0:T(8,128)(2,1)S(1)}, u32[]{:S(2)}, u32[]{:S(2)}) collective-permute-start(bf16[256,1024]{1,0:T(8,128)(2,1)S(1)} %slice.244), channel_id=1, source_target_pairs={{0,8},{8,16},{16,24},{24,0},{32,40},{40,48},{48,56},{56,32},{64,72... | collective-permute-start | bytes 1572872 | tf_op jit(solution)/shard_map/ppermute | solution.py:29
  50.6 14.0 %collective-permute-start.15 = (bf16[256,1024]{1,0:T(8,128)(2,1)S(1)}, bf16[256,1024]{1,0:T(8,128)(2,1)S(1)}, u32[]{:S(2)}, u32[]{:S(2)}) collective-permute-start(bf16[256,1024]{1,0:T(8,128)(2,1)S(1)} %slice.245), channel_id=1, source_target_pairs={{0,24},{8,0},{16,8},{24,16},{32,56},{40,32},{48,40},{56,48},{64,88... | collective-permute-start | bytes 1572872 | tf_op jit(solution)/shard_map/ppermute | solution.py:29
  130.6 16.1 %collective-permute-start.20 = (f16[2,528,256]{2,1,0:T(8,128)(2,1)S(1)}, f16[2,528,256]{2,1,0:T(8,128)(2,1)S(1)}, u32[]{:S(2)}, u32[]{:S(2)}) collective-permute-start(f16[2,528,256]{2,1,0:T(8,128)(2,1)S(1)} %get-tuple-element.69), channel_id=1, source_target_pairs={{0,32},{8,40},{16,48},{24,56},{32,64},{40,72},{48,80},{56,88},{64,... | collective-permute-start | bytes 1622024 | tf_op jit(solution)/shard_map/ppermute | solution.py:29
  131.2 15.6 %collective-permute-start.22 = (f16[2,528,256]{2,1,0:T(8,128)(2,1)S(1)}, f16[2,528,256]{2,1,0:T(8,128)(2,1)S(1)}, u32[]{:S(2)}, u32[]{:S(2)}) collective-permute-start(f16[2,528,256]{2,1,0:T(8,128)(2,1)S(1)} %get-tuple-element.68), channel_id=1, source_target_pairs={{0,96},{8,104},{16,112},{24,120},{32,0},{40,8},{48,16},{56,24},{64... | collective-permute-start | bytes 1622024 | tf_op jit(solution)/shard_map/ppermute | solution.py:29
  136.4 14.2 %collective-permute-start.18 = (f16[2,528,256]{2,1,0:T(8,128)(2,1)S(1)}, f16[2,528,256]{2,1,0:T(8,128)(2,1)S(1)}, u32[]{:S(2)}, u32[]{:S(2)}) collective-permute-start(f16[2,528,256]{2,1,0:T(8,128)(2,1)S(1)} %get-tuple-element.66), channel_id=1, source_target_pairs={{0,24},{8,0},{16,8},{24,16},{32,56},{40,32},{48,40},{56,48},{64,88... | collective-permute-start | bytes 1622024 | tf_op jit(solution)/shard_map/ppermute | solution.py:29
  137.8 14.3 %collective-permute-start.16 = (f16[2,528,256]{2,1,0:T(8,128)(2,1)S(1)}, f16[2,528,256]{2,1,0:T(8,128)(2,1)S(1)}, u32[]{:S(2)}, u32[]{:S(2)}) collective-permute-start(f16[2,528,256]{2,1,0:T(8,128)(2,1)S(1)} %get-tuple-element.67), channel_id=1, source_target_pairs={{0,8},{8,16},{16,24},{24,0},{32,40},{40,48},{48,56},{56,32},{64,72... | collective-permute-start | bytes 1622024 | tf_op jit(solution)/shard_map/ppermute | solution.py:29
  148.7 24.7 %collective-permute-start.23 = (f16[4,528,256]{2,1,0:T(8,128)(2,1)}, f16[4,528,256]{2,1,0:T(8,128)(2,1)}, u32[]{:S(2)}, u32[]{:S(2)}) collective-permute-start(f16[4,528,256]{2,1,0:T(8,128)(2,1)} %get-tuple-element.63), channel_id=1, source_target_pairs={{0,96},{8,104},{16,112},{24,120},{32,0},{40,8},{48,16},{56,24},{64... | collective-permute-start | bytes 3244040 | tf_op jit(solution)/shard_map/ppermute | solution.py:29
  150.6 25.4 %collective-permute-start.21 = (f16[4,528,256]{2,1,0:T(8,128)(2,1)S(1)}, f16[4,528,256]{2,1,0:T(8,128)(2,1)}, u32[]{:S(2)}, u32[]{:S(2)}) collective-permute-start(f16[4,528,256]{2,1,0:T(8,128)(2,1)S(1)} %get-tuple-element.62), channel_id=1, source_target_pairs={{0,32},{8,40},{16,48},{24,56},{32,64},{40,72},{48,80},{56,88},{64,... | collective-permute-start | bytes 3244040 | tf_op jit(solution)/shard_map/ppermute | solution.py:29
  154.2 25.3 %collective-permute-start.17 = (f16[4,528,256]{2,1,0:T(8,128)(2,1)}, f16[4,528,256]{2,1,0:T(8,128)(2,1)}, u32[]{:S(2)}, u32[]{:S(2)}) collective-permute-start(f16[4,528,256]{2,1,0:T(8,128)(2,1)} %get-tuple-element.65), channel_id=1, source_target_pairs={{0,8},{8,16},{16,24},{24,0},{32,40},{40,48},{48,56},{56,32},{64,72... | collective-permute-start | bytes 3244040 | tf_op jit(solution)/shard_map/ppermute | solution.py:29
  154.2 25.3 %collective-permute-start.19 = (f16[4,528,256]{2,1,0:T(8,128)(2,1)}, f16[4,528,256]{2,1,0:T(8,128)(2,1)}, u32[]{:S(2)}, u32[]{:S(2)}) collective-permute-start(f16[4,528,256]{2,1,0:T(8,128)(2,1)} %get-tuple-element.64), channel_id=1, source_target_pairs={{0,24},{8,0},{16,8},{24,16},{32,56},{40,32},{48,40},{56,48},{64,88... | collective-permute-start | bytes 3244040 | tf_op jit(solution)/shard_map/ppermute | solution.py:29
  161.6 2.0 copy-start
  179.5 9.9 %collective-permute-start.29 = (f16[528,256]{1,0:T(8,128)(2,1)S(1)}, f16[528,256]{1,0:T(8,128)(2,1)S(1)}, u32[]{:S(2)}, u32[]{:S(2)}) collective-permute-start(f16[528,256]{1,0:T(8,128)(2,1)S(1)} %get-tuple-element.41), channel_id=1, source_target_pairs={{0,16},{8,24},{16,0},{24,8},{32,48},{40,56},{48,32},{56,40},{64,80... | collective-permute-start | bytes 811016 | tf_op jit(solution)/shard_map/ppermute | solution.py:29
  181.0 11.4 %collective-permute-start.28 = (f16[528,256]{1,0:T(8,128)(2,1)S(1)}, f16[528,256]{1,0:T(8,128)(2,1)S(1)}, u32[]{:S(2)}, u32[]{:S(2)}) collective-permute-start(f16[528,256]{1,0:T(8,128)(2,1)S(1)} %get-tuple-element.40), channel_id=1, source_target_pairs={{0,24},{8,0},{16,8},{24,16},{32,56},{40,32},{48,40},{56,48},{64,88... | collective-permute-start | bytes 811016 | tf_op jit(solution)/shard_map/ppermute | solution.py:29
  182.5 9.9 %collective-permute-start.27 = (f16[528,256]{1,0:T(8,128)(2,1)S(1)}, f16[528,256]{1,0:T(8,128)(2,1)S(1)}, u32[]{:S(2)}, u32[]{:S(2)}) collective-permute-start(f16[528,256]{1,0:T(8,128)(2,1)S(1)} %get-tuple-element.39), channel_id=1, source_target_pairs={{0,8},{8,16},{16,24},{24,0},{32,40},{40,48},{48,56},{56,32},{64,72... | collective-permute-start | bytes 811016 | tf_op jit(solution)/shard_map/ppermute | solution.py:29
  185.6 8.9 %collective-permute-start.24 = (f16[528,256]{1,0:T(8,128)(2,1)S(1)}, f16[528,256]{1,0:T(8,128)(2,1)S(1)}, u32[]{:S(2)}, u32[]{:S(2)}) collective-permute-start(f16[528,256]{1,0:T(8,128)(2,1)S(1)} %get-tuple-element.58), channel_id=1, source_target_pairs={{0,32},{8,40},{16,48},{24,56},{32,64},{40,72},{48,80},{56,88},{64,... | collective-permute-start | bytes 811016 | tf_op jit(solution)/shard_map/ppermute | solution.py:29
  185.7 10.9 %collective-permute-start.25 = (f16[528,256]{1,0:T(8,128)(2,1)S(1)}, f16[528,256]{1,0:T(8,128)(2,1)S(1)}, u32[]{:S(2)}, u32[]{:S(2)}) collective-permute-start(f16[528,256]{1,0:T(8,128)(2,1)S(1)} %get-tuple-element.57), channel_id=1, source_target_pairs={{0,96},{8,104},{16,112},{24,120},{32,0},{40,8},{48,16},{56,24},{64... | collective-permute-start | bytes 811016 | tf_op jit(solution)/shard_map/ppermute | solution.py:29
  189.5 8.0 %collective-permute-start.26 = (f16[528,256]{1,0:T(8,128)(2,1)S(1)}, f16[528,256]{1,0:T(8,128)(2,1)S(1)}, u32[]{:S(2)}, u32[]{:S(2)}) collective-permute-start(f16[528,256]{1,0:T(8,128)(2,1)S(1)} %get-tuple-element.56), channel_id=1, source_target_pairs={{0,64},{8,72},{16,80},{24,88},{32,96},{40,104},{48,112},{56,120},{... | collective-permute-start | bytes 811016 | tf_op jit(solution)/shard_map/ppermute | solution.py:29

commit v3 on v2

--- a/solution.py
+++ b/solution.py
@@ -196,7 +196,7 @@
             part_ref[i, count:] = mass_ref[half]
             return carry
 
-        lax.fori_loop(0, each, body, 0)
+        lax.fori_loop(0, each, body, 0, unroll=each if len(halves) * each == SIDE else 1)
 
 
 def _part(shares, mass, halves, blocks, slots, flops=1000):

time: 200 us -> 200 us (level)
  no operation moved by 1% of the time
where the time goes in v3:
time: 200 us; the launch traced here: 199 us
  blocking collectives  57.5 us (29%)
  starting transfers between devices  47.2 us (24%)
  Pallas kernels  32.3 us (16%)
  waiting for transfers between devices  29.5 us (15%)
  other arithmetic  17.2 us (9%)
  local copies, waits for them, and re-layouts  9.34 us (5%)
  matrix products  5.18 us (3%)
    all_to_all x6, blocking collectives, _exchange(): return lax.all_to_all(copies, axis, 0, 0)  57.5 us
    ppermute x30, starting transfers between devices, _send(): return lax.ppermute(value, 'dp', axis(step))  47.2 us
    ppermute x30, waiting for transfers between devices, _send(): return lax.ppermute(value, 'dp', axis(step))  29.5 us
    pallas_call x5, Pallas kernels, _part(): pl.pallas_call(functools.partial(_part_kernel, halves), in_specs=[pl.Bloc...  15.8 us
    convert_element_type x6, other arithmetic, _pack(): return (value * PACK).astype(jnp.float16)  8.83 us
    unnamed x11, local copies, waits for them, and re-layouts  7.97 us
    pallas_call x2, Pallas kernels, _near_scores(): pl.pallas_call(_near_scores_kernel, grid=(SIDE,), in_specs=[tiles, panel,...  7.19 us
    pallas_call x1, Pallas kernels, _reorder(): pl.pallas_call(_reorder_kernel, grid_spec=pltpu.PrefetchScalarGridSpec(nu...  6.45 us
  transfers between devices with their start and end apart: 30, of which 14 were waited for; matrix products, arithmetic and copies ran while one was open for 10% of the time, Pallas kernels for 14%

profile of v3, /device:TPU:0, one launch (start us, length us, event | category | flops | bytes accessed | tf_op | source)
XLA Modules:
  0.0 199.4 jit_solution(3491915973991276232)
XLA Ops:
  1.7 2.1 %collective-permute-start.1 = (bf16[512,256]{1,0:T(8,128)(2,1)S(1)}, bf16[512,256]{1,0:T(8,128)(2,1)S(1)}, u32[]{:S(2)}, u32[]{:S(2)}) collective-permute-start(bf16[512,256]{1,0:T(8,128)(2,1)S(1)} %get-tuple-element.71), channel_id=1, source_target_pairs={{0,8},{8,16},{16,24},{24,0},{32,40},{40,48},{48,56},{56,32},{64,72... | collective-permute-start | bytes 786440 | tf_op jit(solution)/shard_map/ppermute | solution.py:29
  3.8 2.2 %collective-permute-start = (bf16[512,256]{1,0:T(8,128)(2,1)S(1)}, bf16[512,256]{1,0:T(8,128)(2,1)S(1)}, u32[]{:S(2)}, u32[]{:S(2)}) collective-permute-start(bf16[512,256]{1,0:T(8,128)(2,1)S(1)} %get-tuple-element.71), channel_id=1, source_target_pairs={{0,24},{8,0},{16,8},{24,16},{32,56},{40,32},{48,40},{56,48},{64,88... | collective-permute-start | bytes 786440 | tf_op jit(solution)/shard_map/ppermute | solution.py:29
  9.3 2.4 %collective-permute-done = bf16[512,256]{1,0:T(8,128)(2,1)S(1)} collective-permute-done((bf16[512,256]{1,0:T(8,128)(2,1)S(1)}, bf16[512,256]{1,0:T(8,128)(2,1)S(1)}, u32[]{:S(2)}, u32[]{:S(2)}) %collective-permute-start) | collective-permute-done | bytes 262176 | tf_op jit(solution)/shard_map/ppermute | solution.py:29
  11.7 3.6 %collective-permute-start.3 = (bf16[256,256]{1,0:T(8,128)(2,1)S(1)}, bf16[256,256]{1,0:T(8,128)(2,1)S(1)}, u32[]{:S(2)}, u32[]{:S(2)}) collective-permute-start(bf16[256,256]{1,0:T(8,128)(2,1)S(1)} %slice.239), channel_id=1, source_target_pairs={{0,24},{8,0},{16,8},{24,16},{32,56},{40,32},{48,40},{56,48},{64,88... | collective-permute-start | bytes 393224 | tf_op jit(solution)/shard_map/ppermute | solution.py:29
  15.5 2.8 %collective-permute-start.7 = (bf16[256,256]{1,0:T(8,128)(2,1)S(1)}, bf16[256,256]{1,0:T(8,128)(2,1)S(1)}, u32[]{:S(2)}, u32[]{:S(2)}) collective-permute-start(bf16[256,256]{1,0:T(8,128)(2,1)S(1)} %slice.241), channel_id=1, source_target_pairs={{0,96},{8,104},{16,112},{24,120},{32,0},{40,8},{48,16},{56,24},{64... | collective-permute-start | bytes 393224 | tf_op jit(solution)/shard_map/ppermute | solution.py:29
  18.4 3.2 %collective-permute-done.2 = bf16[256,256]{1,0:T(8,128)(2,1)S(1)} collective-permute-done((bf16[256,256]{1,0:T(8,128)(2,1)S(1)}, bf16[256,256]{1,0:T(8,128)(2,1)S(1)}, u32[]{:S(2)}, u32[]{:S(2)}) %collective-permute-start.2) | collective-permute-done | bytes 131104 | tf_op jit(solution)/shard_map/ppermute | solution.py:29
  26.5 3.2 %collective-permute-start.12 = (bf16[512,1024]{1,0:T(8,128)(2,1)S(1)}, bf16[512,1024]{1,0:T(8,128)(2,1)S(1)}, u32[]{:S(2)}, u32[]{:S(2)}) collective-permute-start(bf16[512,1024]{1,0:T(8,128)(2,1)S(1)} %get-tuple-element.53), channel_id=1, source_target_pairs={{0,24},{8,0},{16,8},{24,16},{32,56},{40,32},{48,40},{56,48},{64,88... | collective-permute-start | bytes 3145736 | tf_op jit(solution)/shard_map/ppermute | solution.py:29
  29.9 3.4 %copy-done.1 = bf16[1024,4096]{1,0:T(8,128)(2,1)S(1)} copy-done((bf16[1024,4096]{1,0:T(8,128)(2,1)S(1)}, bf16[1024,4096]{1,0:T(8,128)(2,1)}, u32[]{:S(2)}) %copy-start.1) | copy-done | bytes 8388632
  33.3 6.5 %shard_map.41 = (bf16[1024,4096]{1,0:T(8,128)(2,1)S(1)}, bf16[1024,4096]{1,0:T(8,128)(2,1)S(1)}, bf16[16,1024,256]{2,1,0:T(8,128)(2,1)S(1)}) custom-call(s32[2]{0:T(128)S(1)} %pad_add_fusion.place_ref, bf16[1024,4096]{1,0:T(8,128)(2,1)S(1)} %copy-done.1), custom_call_target="tpu_custom_call" | custom-call | flops 12582912 | bytes 33554432 | tf_op jit(solution)/shard_map/pallas_call | solution.py:296
  42.3 4.7 %collective-permute-done.9.before_ref = bf16[512,1024]{1,0:T(8,128)(2,1)S(1)} collective-permute-done((bf16[512,1024]{1,0:T(8,128)(2,1)S(1)}, bf16[512,1024]{1,0:T(8,128)(2,1)S(1)}, u32[]{:S(2)}, u32[]{:S(2)}) %collective-permute-start.9) | collective-permute-done | bytes 1048608 | tf_op jit(solution)/shard_map/ppermute | solution.py:29
  47.2 3.3 %collective-permute-start.11 = (bf16[256,1024]{1,0:T(8,128)(2,1)S(1)}, bf16[256,1024]{1,0:T(8,128)(2,1)S(1)}, u32[]{:S(2)}, u32[]{:S(2)}) collective-permute-start(bf16[256,1024]{1,0:T(8,128)(2,1)S(1)} %slice.243), channel_id=1, source_target_pairs={{0,96},{8,104},{16,112},{24,120},{32,0},{40,8},{48,16},{56,24},{64... | collective-permute-start | bytes 1572872 | tf_op jit(solution)/shard_map/ppermute | solution.py:29
  50.6 3.5 %collective-permute-start.15 = (bf16[256,1024]{1,0:T(8,128)(2,1)S(1)}, bf16[256,1024]{1,0:T(8,128)(2,1)S(1)}, u32[]{:S(2)}, u32[]{:S(2)}) collective-permute-start(bf16[256,1024]{1,0:T(8,128)(2,1)S(1)} %slice.245), channel_id=1, source_target_pairs={{0,24},{8,0},{16,8},{24,16},{32,56},{40,32},{48,40},{56,48},{64,88... | collective-permute-start | bytes 1572872 | tf_op jit(solution)/shard_map/ppermute | solution.py:29
  54.7 3.6 %shard_map.42 = f32[512,1024]{1,0:T(8,128)S(1)} custom-call(f32[512,1024]{1,0:T(8,128)S(1)} %fusion.14.total_ref, bf16[512,1024]{1,0:T(8,128)(2,1)S(1)} %collective-permute-done.8.after_ref, bf16[512,1024]{1,0:T(8,128)(2,1)S(1)} %collective-permute-done.9.before_ref, bf16[1024,4096]{1,0:T(8,128)(2,1)S(1)} %get-tuple-element.25.rows_1_ref.rows_3_ref, ...), custom_call_target="tpu_custom_call" | custom-call | flops 2147483648 | bytes 10485760 | tf_op jit(solution)/shard_map/pallas_call | solution.py:67
  58.8 3.6 %shard_map.43 = f32[512,1024]{1,0:T(8,128)S(1)} custom-call(f32[512,1024]{1,0:T(8,128)S(1)} %fusion.10.total_ref, bf16[512,1024]{1,0:T(8,128)(2,1)S(1)} %collective-permute-done.12.after_ref, bf16[512,1024]{1,0:T(8,128)(2,1)S(1)} %collective-permute-done.13.before_ref, bf16[1024,4096]{1,0:T(8,128)(2,1)S(1)} %get-tuple-element.26.rows_1_ref.rows_3_ref, ...), custom_call_target="tpu_custom_call" | custom-call | flops 2147483648 | bytes 10485760 | tf_op jit(solution)/shard_map/pallas_call | solution.py:67
  67.6 10.4 %all_to_all.30.column_ref = f32[16,1,1024]{2,1,0:T(1,128)S(1)} all-to-all(f32[16,1,1024]{2,1,0:T(1,128)S(1)} %broadcast_in_dim.2), channel_id=1, replica_groups=mesh['dp'=16,'cent'=8] {'dp'}, dimensions={0} | all-to-all | bytes 131072 | tf_op jit(solution)/shard_map/all_to_all | solution.py:182
  78.4 9.7 %all_to_all.31.row_ref = f32[8,1,1024]{2,1,0:T(1,128)S(1)} all-to-all(f32[8,1,1024]{2,1,0:T(1,128)S(1)} %shard_map.44), channel_id=1, replica_groups=mesh['dp'=16,'cent'=8] {'cent'}, dimensions={0} | all-to-all | bytes 65536 | tf_op jit(solution)/shard_map/all_to_all | solution.py:182
  88.5 10.9 %all_to_all.32.column_ref = f32[16,1,1024]{2,1,0:T(1,128)S(1)} all-to-all(f32[16,1,1024]{2,1,0:T(1,128)S(1)} %shard_map.45), channel_id=1, replica_groups=mesh['dp'=16,'cent'=8] {'dp'}, dimensions={0} | all-to-all | bytes 131072 | tf_op jit(solution)/shard_map/all_to_all | solution.py:182
  99.8 7.8 %all_to_all.33.row_ref = f32[8,1,1024]{2,1,0:T(1,128)S(1)} all-to-all(f32[8,1,1024]{2,1,0:T(1,128)S(1)} %shard_map.46), channel_id=1, replica_groups=mesh['dp'=16,'cent'=8] {'cent'}, dimensions={0} | all-to-all | bytes 65536 | tf_op jit(solution)/shard_map/all_to_all | solution.py:182
  108.0 10.9 %all_to_all.34.column_ref = f32[16,1,1024]{2,1,0:T(1,128)S(1)} all-to-all(f32[16,1,1024]{2,1,0:T(1,128)S(1)} %shard_map.47), channel_id=1, replica_groups=mesh['dp'=16,'cent'=8] {'dp'}, dimensions={0} | all-to-all | bytes 131072 | tf_op jit(solution)/shard_map/all_to_all | solution.py:182
  119.3 7.8 %all_to_all.35.row_ref = f32[8,1,1024]{2,1,0:T(1,128)S(1)} all-to-all(f32[8,1,1024]{2,1,0:T(1,128)S(1)} %shard_map.48), channel_id=1, replica_groups=mesh['dp'=16,'cent'=8] {'cent'}, dimensions={0} | all-to-all | bytes 65536 | tf_op jit(solution)/shard_map/all_to_all | solution.py:182
  130.7 2.7 %collective-permute-start.22 = (f16[2,528,256]{2,1,0:T(8,128)(2,1)S(1)}, f16[2,528,256]{2,1,0:T(8,128)(2,1)S(1)}, u32[]{:S(2)}, u32[]{:S(2)}) collective-permute-start(f16[2,528,256]{2,1,0:T(8,128)(2,1)S(1)} %get-tuple-element.68), channel_id=1, source_target_pairs={{0,96},{8,104},{16,112},{24,120},{32,0},{40,8},{48,16},{56,24},{64... | collective-permute-start | bytes 1622024 | tf_op jit(solution)/shard_map/ppermute | solution.py:29
  137.5 4.1 %shard_map.53 = f32[8,528,256]{2,1,0:T(8,128)S(1)} custom-call(s32[8]{0:T(128)S(1)} %pad_add_fusion.2.slots_ref, bf16[1024,1024]{1,0:T(8,128)(2,1)S(1)} %get-tuple-element.34.shares_ref, f32[2,16,256]{2,1,0:T(8,128)S(1)} %get-tuple-element.31.mass_ref, bf16[16,1024,256]{2,1,0:T(8,128)(2,1)S(1)} %get-tuple-element.32.rows_ref), custom_call_target="tpu_custom_call" | custom-call | flops 1000 | bytes 1 | tf_op jit(solution)/shard_map/pallas_call | solution.py:206
  141.6 4.1 %shard_map.54 = f32[8,528,256]{2,1,0:T(8,128)S(1)} custom-call(s32[8]{0:T(128)S(1)} %pad_add_fusion.1.slots_ref, bf16[1024,1024]{1,0:T(8,128)(2,1)S(1)} %get-tuple-element.34.shares_ref, f32[2,16,256]{2,1,0:T(8,128)S(1)} %get-tuple-element.31.mass_ref, bf16[16,1024,256]{2,1,0:T(8,128)(2,1)S(1)} %get-tuple-element.32.rows_ref), custom_call_target="tpu_custom_call" | custom-call | flops 1000 | bytes 1 | tf_op jit(solution)/shard_map/pallas_call | solution.py:206
  147.6 2.5 %collective-permute-start.23 = (f16[4,528,256]{2,1,0:T(8,128)(2,1)}, f16[4,528,256]{2,1,0:T(8,128)(2,1)}, u32[]{:S(2)}, u32[]{:S(2)}) collective-permute-start(f16[4,528,256]{2,1,0:T(8,128)(2,1)} %get-tuple-element.63), channel_id=1, source_target_pairs={{0,96},{8,104},{16,112},{24,120},{32,0},{40,8},{48,16},{56,24},{64... | collective-permute-start | bytes 3244040 | tf_op jit(solution)/shard_map/ppermute | solution.py:29
  153.2 3.2 %collective-permute-start.19 = (f16[4,528,256]{2,1,0:T(8,128)(2,1)}, f16[4,528,256]{2,1,0:T(8,128)(2,1)}, u32[]{:S(2)}, u32[]{:S(2)}) collective-permute-start(f16[4,528,256]{2,1,0:T(8,128)(2,1)} %get-tuple-element.64), channel_id=1, source_target_pairs={{0,24},{8,0},{16,8},{24,16},{32,56},{40,32},{48,40},{56,48},{64,88... | collective-permute-start | bytes 3244040 | tf_op jit(solution)/shard_map/ppermute | solution.py:29
  156.5 4.1 %shard_map.52 = f32[8,528,256]{2,1,0:T(8,128)S(1)} custom-call(s32[8]{0:T(128)S(1)} %pad_add_fusion.3.slots_ref, bf16[1024,1024]{1,0:T(8,128)(2,1)S(1)} %get-tuple-element.34.shares_ref, f32[2,16,256]{2,1,0:T(8,128)S(1)} %get-tuple-element.31.mass_ref, bf16[16,1024,256]{2,1,0:T(8,128)(2,1)S(1)} %get-tuple-element.32.rows_ref), custom_call_target="tpu_custom_call" | custom-call | flops 1000 | bytes 1 | tf_op jit(solution)/shard_map/pallas_call | solution.py:206
  162.6 2.5 %copy.4 = bf16[1024,1024]{1,0:T(8,128)(2,1)} copy(bf16[1024,1024]{0,1:T(8,128)(2,1)S(1)} %bitcast.57) | data formatting | bytes 4194304
  165.1 7.3 %collective-permute-done.23 = f16[4,528,256]{2,1,0:T(8,128)(2,1)} collective-permute-done((f16[4,528,256]{2,1,0:T(8,128)(2,1)}, f16[4,528,256]{2,1,0:T(8,128)(2,1)}, u32[]{:S(2)}, u32[]{:S(2)}) %collective-permute-start.23) | collective-permute-done | bytes 1081376 | tf_op jit(solution)/shard_map/ppermute | solution.py:29
  172.4 3.1 %collective-permute-done.21 = f16[4,528,256]{2,1,0:T(8,128)(2,1)} collective-permute-done((f16[4,528,256]{2,1,0:T(8,128)(2,1)S(1)}, f16[4,528,256]{2,1,0:T(8,128)(2,1)}, u32[]{:S(2)}, u32[]{:S(2)}) %collective-permute-start.21) | collective-permute-done | bytes 1081376 | tf_op jit(solution)/shard_map/ppermute | solution.py:29
  175.5 2.3 %fusion.53 = (f16[528,256]{1,0:T(8,128)(2,1)S(1)}, f16[528,256]{1,0:T(8,128)(2,1)S(1)}, f16[528,256]{1,0:T(8,128)(2,1)S(1)}) fusion(f32[8,528,256]{2,1,0:T(8,128)} %copy-done, f16[4,528,256]{2,1,0:T(8,128)(2,1)} %collective-permute-done.23, f16[4,528,256]{2,1,0:T(8,128)(2,1)} %collective-permute-done.21), kind=kLoop, calls=%fused_computation.88 | loop fusion | flops 3244032 | bytes 4055040 | tf_op jit(solution)/shard_map/convert_element_type | solution.py:100
  182.3 2.3 %fusion.55 = (f16[528,256]{1,0:T(8,128)(2,1)S(1)}, f16[528,256]{1,0:T(8,128)(2,1)S(1)}, f16[528,256]{1,0:T(8,128)(2,1)S(1)}) fusion(f32[8,528,256]{2,1,0:T(8,128)} %copy-done, f16[4,528,256]{2,1,0:T(8,128)(2,1)} %collective-permute-done.19, f16[4,528,256]{2,1,0:T(8,128)(2,1)} %collective-permute-done.17), kind=kLoop, calls=%fused_computation.90 | loop fusion | flops 3244032 | bytes 4055040 | tf_op jit(solution)/shard_map/convert_element_type | solution.py:100
  184.7 3.2 %collective-permute-start.25 = (f16[528,256]{1,0:T(8,128)(2,1)S(1)}, f16[528,256]{1,0:T(8,128)(2,1)S(1)}, u32[]{:S(2)}, u32[]{:S(2)}) collective-permute-start(f16[528,256]{1,0:T(8,128)(2,1)S(1)} %get-tuple-element.57), channel_id=1, source_target_pairs={{0,96},{8,104},{16,112},{24,120},{32,0},{40,8},{48,16},{56,24},{64... | collective-permute-start | bytes 811016 | tf_op jit(solution)/shard_map/ppermute | solution.py:29
  (111 shorter events, 51.5 us)
Async XLA Ops:
  1.7 13.6 %collective-permute-start.1 = (bf16[512,256]{1,0:T(8,128)(2,1)S(1)}, bf16[512,256]{1,0:T(8,128)(2,1)S(1)}, u32[]{:S(2)}, u32[]{:S(2)}) collective-permute-start(bf16[512,256]{1,0:T(8,128)(2,1)S(1)} %get-tuple-element.71), channel_id=1, source_target_pairs={{0,8},{8,16},{16,24},{24,0},{32,40},{40,48},{48,56},{56,32},{64,72... | collective-permute-start | bytes 786440 | tf_op jit(solution)/shard_map/ppermute | solution.py:29
  3.8 7.9 %collective-permute-start = (bf16[512,256]{1,0:T(8,128)(2,1)S(1)}, bf16[512,256]{1,0:T(8,128)(2,1)S(1)}, u32[]{:S(2)}, u32[]{:S(2)}) collective-permute-start(bf16[512,256]{1,0:T(8,128)(2,1)S(1)} %get-tuple-element.71), channel_id=1, source_target_pairs={{0,24},{8,0},{16,8},{24,16},{32,56},{40,32},{48,40},{56,48},{64,88... | collective-permute-start | bytes 786440 | tf_op jit(solution)/shard_map/ppermute | solution.py:29
  6.0 12.3 %collective-permute-start.5 = (bf16[512,256]{1,0:T(8,128)(2,1)S(1)}, bf16[512,256]{1,0:T(8,128)(2,1)S(1)}, u32[]{:S(2)}, u32[]{:S(2)}) collective-permute-start(bf16[512,256]{1,0:T(8,128)(2,1)S(1)} %get-tuple-element.70), channel_id=1, source_target_pairs={{0,32},{8,40},{16,48},{24,56},{32,64},{40,72},{48,80},{56,88},{64,... | collective-permute-start | bytes 786440 | tf_op jit(solution)/shard_map/ppermute | solution.py:29
  7.5 8.0 %collective-permute-start.4 = (bf16[512,256]{1,0:T(8,128)(2,1)S(1)}, bf16[512,256]{1,0:T(8,128)(2,1)S(1)}, u32[]{:S(2)}, u32[]{:S(2)}) collective-permute-start(bf16[512,256]{1,0:T(8,128)(2,1)S(1)} %get-tuple-element.70), channel_id=1, source_target_pairs={{0,96},{8,104},{16,112},{24,120},{32,0},{40,8},{48,16},{56,24},{64... | collective-permute-start | bytes 786440 | tf_op jit(solution)/shard_map/ppermute | solution.py:29
  11.7 6.7 %collective-permute-start.3 = (bf16[256,256]{1,0:T(8,128)(2,1)S(1)}, bf16[256,256]{1,0:T(8,128)(2,1)S(1)}, u32[]{:S(2)}, u32[]{:S(2)}) collective-permute-start(bf16[256,256]{1,0:T(8,128)(2,1)S(1)} %slice.239), channel_id=1, source_target_pairs={{0,24},{8,0},{16,8},{24,16},{32,56},{40,32},{48,40},{56,48},{64,88... | collective-permute-start | bytes 393224 | tf_op jit(solution)/shard_map/ppermute | solution.py:29
  15.3 6.2 %collective-permute-start.2 = (bf16[256,256]{1,0:T(8,128)(2,1)S(1)}, bf16[256,256]{1,0:T(8,128)(2,1)S(1)}, u32[]{:S(2)}, u32[]{:S(2)}) collective-permute-start(bf16[256,256]{1,0:T(8,128)(2,1)S(1)} %slice.238), channel_id=1, source_target_pairs={{0,8},{8,16},{16,24},{24,0},{32,40},{40,48},{48,56},{56,32},{64,72... | collective-permute-start | bytes 393224 | tf_op jit(solution)/shard_map/ppermute | solution.py:29
  15.5 9.7 %collective-permute-start.7 = (bf16[256,256]{1,0:T(8,128)(2,1)S(1)}, bf16[256,256]{1,0:T(8,128)(2,1)S(1)}, u32[]{:S(2)}, u32[]{:S(2)}) collective-permute-start(bf16[256,256]{1,0:T(8,128)(2,1)S(1)} %slice.241), channel_id=1, source_target_pairs={{0,96},{8,104},{16,112},{24,120},{32,0},{40,8},{48,16},{56,24},{64... | collective-permute-start | bytes 393224 | tf_op jit(solution)/shard_map/ppermute | solution.py:29
  18.3 7.5 %collective-permute-start.6 = (bf16[256,256]{1,0:T(8,128)(2,1)S(1)}, bf16[256,256]{1,0:T(8,128)(2,1)S(1)}, u32[]{:S(2)}, u32[]{:S(2)}) collective-permute-start(bf16[256,256]{1,0:T(8,128)(2,1)S(1)} %slice.240), channel_id=1, source_target_pairs={{0,32},{8,40},{16,48},{24,56},{32,64},{40,72},{48,80},{56,88},{64,... | collective-permute-start | bytes 393224 | tf_op jit(solution)/shard_map/ppermute | solution.py:29
  21.9 25.2 %collective-permute-start.9 = (bf16[512,1024]{1,0:T(8,128)(2,1)S(1)}, bf16[512,1024]{1,0:T(8,128)(2,1)S(1)}, u32[]{:S(2)}, u32[]{:S(2)}) collective-permute-start(bf16[512,1024]{1,0:T(8,128)(2,1)S(1)} %get-tuple-element.55), channel_id=1, source_target_pairs={{0,32},{8,40},{16,48},{24,56},{32,64},{40,72},{48,80},{56,88},{64,... | collective-permute-start | bytes 3145736 | tf_op jit(solution)/shard_map/ppermute | solution.py:29
  23.4 23.7 %collective-permute-start.8 = (bf16[512,1024]{1,0:T(8,128)(2,1)S(1)}, bf16[512,1024]{1,0:T(8,128)(2,1)S(1)}, u32[]{:S(2)}, u32[]{:S(2)}) collective-permute-start(bf16[512,1024]{1,0:T(8,128)(2,1)S(1)} %get-tuple-element.55), channel_id=1, source_target_pairs={{0,96},{8,104},{16,112},{24,120},{32,0},{40,8},{48,16},{56,24},{64... | collective-permute-start | bytes 3145736 | tf_op jit(solution)/shard_map/ppermute | solution.py:29
  26.1 24.4 %collective-permute-start.13 = (bf16[512,1024]{1,0:T(8,128)(2,1)S(1)}, bf16[512,1024]{1,0:T(8,128)(2,1)S(1)}, u32[]{:S(2)}, u32[]{:S(2)}) collective-permute-start(bf16[512,1024]{1,0:T(8,128)(2,1)S(1)} %get-tuple-element.53), channel_id=1, source_target_pairs={{0,8},{8,16},{16,24},{24,0},{32,40},{40,48},{48,56},{56,32},{64,72... | collective-permute-start | bytes 3145736 | tf_op jit(solution)/shard_map/ppermute | solution.py:29
  26.5 24.1 %collective-permute-start.12 = (bf16[512,1024]{1,0:T(8,128)(2,1)S(1)}, bf16[512,1024]{1,0:T(8,128)(2,1)S(1)}, u32[]{:S(2)}, u32[]{:S(2)}) collective-permute-start(bf16[512,1024]{1,0:T(8,128)(2,1)S(1)} %get-tuple-element.53), channel_id=1, source_target_pairs={{0,24},{8,0},{16,8},{24,16},{32,56},{40,32},{48,40},{56,48},{64,88... | collective-permute-start | bytes 3145736 | tf_op jit(solution)/shard_map/ppermute | solution.py:29
  29.9 3.4 %copy-start.1 = (bf16[1024,4096]{1,0:T(8,128)(2,1)S(1)}, bf16[1024,4096]{1,0:T(8,128)(2,1)}, u32[]{:S(2)}) copy-start(bf16[1024,4096]{1,0:T(8,128)(2,1)} %rows_ref.1) | copy-start | bytes 25165828
  47.1 15.4 %collective-permute-start.10 = (bf16[256,1024]{1,0:T(8,128)(2,1)S(1)}, bf16[256,1024]{1,0:T(8,128)(2,1)S(1)}, u32[]{:S(2)}, u32[]{:S(2)}) collective-permute-start(bf16[256,1024]{1,0:T(8,128)(2,1)S(1)} %slice.242), channel_id=1, source_target_pairs={{0,32},{8,40},{16,48},{24,56},{32,64},{40,72},{48,80},{56,88},{64,... | collective-permute-start | bytes 1572872 | tf_op jit(solution)/shard_map/ppermute | solution.py:29
  47.2 15.8 %collective-permute-start.11 = (bf16[256,1024]{1,0:T(8,128)(2,1)S(1)}, bf16[256,1024]{1,0:T(8,128)(2,1)S(1)}, u32[]{:S(2)}, u32[]{:S(2)}) collective-permute-start(bf16[256,1024]{1,0:T(8,128)(2,1)S(1)} %slice.243), channel_id=1, source_target_pairs={{0,96},{8,104},{16,112},{24,120},{32,0},{40,8},{48,16},{56,24},{64... | collective-permute-start | bytes 1572872 | tf_op jit(solution)/shard_map/ppermute | solution.py:29
  50.5 12.4 %collective-permute-start.14 = (bf16[256,1024]{1,0:T(8,128)(2,1)S(1)}, bf16[256,1024]{1,0:T(8,128)(2,1)S(1)}, u32[]{:S(2)}, u32[]{:S(2)}) collective-permute-start(bf16[256,1024]{1,0:T(8,128)(2,1)S(1)} %slice.244), channel_id=1, source_target_pairs={{0,8},{8,16},{16,24},{24,0},{32,40},{40,48},{48,56},{56,32},{64,72... | collective-permute-start | bytes 1572872 | tf_op jit(solution)/shard_map/ppermute | solution.py:29
  50.6 14.0 %collective-permute-start.15 = (bf16[256,1024]{1,0:T(8,128)(2,1)S(1)}, bf16[256,1024]{1,0:T(8,128)(2,1)S(1)}, u32[]{:S(2)}, u32[]{:S(2)}) collective-permute-start(bf16[256,1024]{1,0:T(8,128)(2,1)S(1)} %slice.245), channel_id=1, source_target_pairs={{0,24},{8,0},{16,8},{24,16},{32,56},{40,32},{48,40},{56,48},{64,88... | collective-permute-start | bytes 1572872 | tf_op jit(solution)/shard_map/ppermute | solution.py:29
  130.1 15.6 %collective-permute-start.20 = (f16[2,528,256]{2,1,0:T(8,128)(2,1)S(1)}, f16[2,528,256]{2,1,0:T(8,128)(2,1)S(1)}, u32[]{:S(2)}, u32[]{:S(2)}) collective-permute-start(f16[2,528,256]{2,1,0:T(8,128)(2,1)S(1)} %get-tuple-element.69), channel_id=1, source_target_pairs={{0,32},{8,40},{16,48},{24,56},{32,64},{40,72},{48,80},{56,88},{64,... | collective-permute-start | bytes 1622024 | tf_op jit(solution)/shard_map/ppermute | solution.py:29
  130.7 15.1 %collective-permute-start.22 = (f16[2,528,256]{2,1,0:T(8,128)(2,1)S(1)}, f16[2,528,256]{2,1,0:T(8,128)(2,1)S(1)}, u32[]{:S(2)}, u32[]{:S(2)}) collective-permute-start(f16[2,528,256]{2,1,0:T(8,128)(2,1)S(1)} %get-tuple-element.68), channel_id=1, source_target_pairs={{0,96},{8,104},{16,112},{24,120},{32,0},{40,8},{48,16},{56,24},{64... | collective-permute-start | bytes 1622024 | tf_op jit(solution)/shard_map/ppermute | solution.py:29
  135.4 14.7 %collective-permute-start.18 = (f16[2,528,256]{2,1,0:T(8,128)(2,1)S(1)}, f16[2,528,256]{2,1,0:T(8,128)(2,1)S(1)}, u32[]{:S(2)}, u32[]{:S(2)}) collective-permute-start(f16[2,528,256]{2,1,0:T(8,128)(2,1)S(1)} %get-tuple-element.66), channel_id=1, source_target_pairs={{0,24},{8,0},{16,8},{24,16},{32,56},{40,32},{48,40},{56,48},{64,88... | collective-permute-start | bytes 1622024 | tf_op jit(solution)/shard_map/ppermute | solution.py:29
  136.7 14.3 %collective-permute-start.16 = (f16[2,528,256]{2,1,0:T(8,128)(2,1)S(1)}, f16[2,528,256]{2,1,0:T(8,128)(2,1)S(1)}, u32[]{:S(2)}, u32[]{:S(2)}) collective-permute-start(f16[2,528,256]{2,1,0:T(8,128)(2,1)S(1)} %get-tuple-element.67), channel_id=1, source_target_pairs={{0,8},{8,16},{16,24},{24,0},{32,40},{40,48},{48,56},{56,32},{64,72... | collective-permute-start | bytes 1622024 | tf_op jit(solution)/shard_map/ppermute | solution.py:29
  147.6 24.7 %collective-permute-start.23 = (f16[4,528,256]{2,1,0:T(8,128)(2,1)}, f16[4,528,256]{2,1,0:T(8,128)(2,1)}, u32[]{:S(2)}, u32[]{:S(2)}) collective-permute-start(f16[4,528,256]{2,1,0:T(8,128)(2,1)} %get-tuple-element.63), channel_id=1, source_target_pairs={{0,96},{8,104},{16,112},{24,120},{32,0},{40,8},{48,16},{56,24},{64... | collective-permute-start | bytes 3244040 | tf_op jit(solution)/shard_map/ppermute | solution.py:29
  150.1 25.4 %collective-permute-start.21 = (f16[4,528,256]{2,1,0:T(8,128)(2,1)S(1)}, f16[4,528,256]{2,1,0:T(8,128)(2,1)}, u32[]{:S(2)}, u32[]{:S(2)}) collective-permute-start(f16[4,528,256]{2,1,0:T(8,128)(2,1)S(1)} %get-tuple-element.62), channel_id=1, source_target_pairs={{0,32},{8,40},{16,48},{24,56},{32,64},{40,72},{48,80},{56,88},{64,... | collective-permute-start | bytes 3244040 | tf_op jit(solution)/shard_map/ppermute | solution.py:29
  153.2 25.3 %collective-permute-start.17 = (f16[4,528,256]{2,1,0:T(8,128)(2,1)}, f16[4,528,256]{2,1,0:T(8,128)(2,1)}, u32[]{:S(2)}, u32[]{:S(2)}) collective-permute-start(f16[4,528,256]{2,1,0:T(8,128)(2,1)} %get-tuple-element.65), channel_id=1, source_target_pairs={{0,8},{8,16},{16,24},{24,0},{32,40},{40,48},{48,56},{56,32},{64,72... | collective-permute-start | bytes 3244040 | tf_op jit(solution)/shard_map/ppermute | solution.py:29
  153.2 25.3 %collective-permute-start.19 = (f16[4,528,256]{2,1,0:T(8,128)(2,1)}, f16[4,528,256]{2,1,0:T(8,128)(2,1)}, u32[]{:S(2)}, u32[]{:S(2)}) collective-permute-start(f16[4,528,256]{2,1,0:T(8,128)(2,1)} %get-tuple-element.64), channel_id=1, source_target_pairs={{0,24},{8,0},{16,8},{24,16},{32,56},{40,32},{48,40},{56,48},{64,88... | collective-permute-start | bytes 3244040 | tf_op jit(solution)/shard_map/ppermute | solution.py:29
  160.6 2.0 copy-start
  178.5 9.9 %collective-permute-start.29 = (f16[528,256]{1,0:T(8,128)(2,1)S(1)}, f16[528,256]{1,0:T(8,128)(2,1)S(1)}, u32[]{:S(2)}, u32[]{:S(2)}) collective-permute-start(f16[528,256]{1,0:T(8,128)(2,1)S(1)} %get-tuple-element.41), channel_id=1, source_target_pairs={{0,16},{8,24},{16,0},{24,8},{32,48},{40,56},{48,32},{56,40},{64,80... | collective-permute-start | bytes 811016 | tf_op jit(solution)/shard_map/ppermute | solution.py:29
  180.0 11.4 %collective-permute-start.28 = (f16[528,256]{1,0:T(8,128)(2,1)S(1)}, f16[528,256]{1,0:T(8,128)(2,1)S(1)}, u32[]{:S(2)}, u32[]{:S(2)}) collective-permute-start(f16[528,256]{1,0:T(8,128)(2,1)S(1)} %get-tuple-element.40), channel_id=1, source_target_pairs={{0,24},{8,0},{16,8},{24,16},{32,56},{40,32},{48,40},{56,48},{64,88... | collective-permute-start | bytes 811016 | tf_op jit(solution)/shard_map/ppermute | solution.py:29
  181.5 9.9 %collective-permute-start.27 = (f16[528,256]{1,0:T(8,128)(2,1)S(1)}, f16[528,256]{1,0:T(8,128)(2,1)S(1)}, u32[]{:S(2)}, u32[]{:S(2)}) collective-permute-start(f16[528,256]{1,0:T(8,128)(2,1)S(1)} %get-tuple-element.39), channel_id=1, source_target_pairs={{0,8},{8,16},{16,24},{24,0},{32,40},{40,48},{48,56},{56,32},{64,72... | collective-permute-start | bytes 811016 | tf_op jit(solution)/shard_map/ppermute | solution.py:29
  184.6 9.5 %collective-permute-start.24 = (f16[528,256]{1,0:T(8,128)(2,1)S(1)}, f16[528,256]{1,0:T(8,128)(2,1)S(1)}, u32[]{:S(2)}, u32[]{:S(2)}) collective-permute-start(f16[528,256]{1,0:T(8,128)(2,1)S(1)} %get-tuple-element.58), channel_id=1, source_target_pairs={{0,32},{8,40},{16,48},{24,56},{32,64},{40,72},{48,80},{56,88},{64,... | collective-permute-start | bytes 811016 | tf_op jit(solution)/shard_map/ppermute | solution.py:29
  184.7 10.9 %collective-permute-start.25 = (f16[528,256]{1,0:T(8,128)(2,1)S(1)}, f16[528,256]{1,0:T(8,128)(2,1)S(1)}, u32[]{:S(2)}, u32[]{:S(2)}) collective-permute-start(f16[528,256]{1,0:T(8,128)(2,1)S(1)} %get-tuple-element.57), channel_id=1, source_target_pairs={{0,96},{8,104},{16,112},{24,120},{32,0},{40,8},{48,16},{56,24},{64... | collective-permute-start | bytes 811016 | tf_op jit(solution)/shard_map/ppermute | solution.py:29
  188.4 8.5 %collective-permute-start.26 = (f16[528,256]{1,0:T(8,128)(2,1)S(1)}, f16[528,256]{1,0:T(8,128)(2,1)S(1)}, u32[]{:S(2)}, u32[]{:S(2)}) collective-permute-start(f16[528,256]{1,0:T(8,128)(2,1)S(1)} %get-tuple-element.56), channel_id=1, source_target_pairs={{0,64},{8,72},{16,80},{24,88},{32,96},{40,104},{48,112},{56,120},{... | collective-permute-start | bytes 811016 | tf_op jit(solution)/shard_map/ppermute | solution.py:29
